TPU v7x, 32 devices: a whole 2x2x4 slice. The times are simulated.
32 devices in a mesh: row: 16 (over z, x, core), col: 2 (over y).
Axes of the slice: x: 2, y: 2, z: 4, core: 2. Of those that a mesh axis runs over, the one named last changes fastest.
Arguments:
- s_matrix: bfloat16 [2, 8192, 32768], P(None, 'row', 'col'), may hold values from -0.03125 to 0.03125
- slab: bfloat16 [2, 32768, 384], P(None, ('col', 'row')), may hold values from -6 to 6
- beam_hkl: int32 [3, 32768], P(None, ('col', 'row')), may hold values from -24 to 24
Outputs:
- squared: bfloat16 [2, 8192, 384], P(None, 'row', 'col')
All inputs are finite; a program needn't handle non-finite values.
Results may differ from a plain program's by a relative error of at most 0.014.
Values may be sent and summed in bfloat16 or wider, within the bound.
No kernel may reach another device: no remote copies, remote signals or barrier semaphores. Data moves between devices by JAX's collectives and lax.ppermute only.
A program may use at most 128 MiB of HBM per device.

v0:
```python
import jax
import jax.numpy as jnp
from jax import lax
from jax.sharding import PartitionSpec as P


def apply_phase(slab, beam_hkl):
    hkl_float = beam_hkl.astype(jnp.float32)
    angles = (
        0.61
        * (hkl_float[0] * hkl_float[0] + hkl_float[1] * hkl_float[1] + hkl_float[2] * hkl_float[2])
        + 0.29 * hkl_float[0]
        - 0.17 * hkl_float[1]
        + 0.43 * hkl_float[2]
    )
    cosine = jnp.cos(angles)[:, None]
    sine = jnp.sin(angles)[:, None]
    slab_real = slab[0].astype(jnp.float32)
    slab_imag = slab[1].astype(jnp.float32)
    phased_real = cosine * slab_real - sine * slab_imag
    phased_imag = cosine * slab_imag + sine * slab_real
    return jnp.stack([phased_real, phased_imag]).astype(jnp.bfloat16)


def per_device(s_matrix, slab, beam_hkl):
    phased = apply_phase(slab, beam_hkl)
    gathered = lax.all_gather(phased, "row", axis=1, tiled=True)
    s_real = s_matrix[0]
    s_imag = s_matrix[1]
    part_real = jnp.dot(s_real, gathered[0], preferred_element_type=jnp.float32) - jnp.dot(
        s_imag, gathered[1], preferred_element_type=jnp.float32
    )
    part_imag = jnp.dot(s_real, gathered[1], preferred_element_type=jnp.float32) + jnp.dot(
        s_imag, gathered[0], preferred_element_type=jnp.float32
    )
    totals = jnp.stack([part_real, part_imag])
    return lax.psum_scatter(totals.astype(jnp.bfloat16), "col", scatter_dimension=2, tiled=True)


def solution(mesh):
    placed = (P(None, "row", "col"), P(None, ("col", "row"), None), P(None, ("col", "row")))
    return jax.shard_map(
        per_device, mesh=mesh, in_specs=placed, out_specs=P(None, "row", "col"), check_vma=False
    )
```

profile of v0, /device:TPU:0, one launch (start us, length us, event | category | flops | bytes accessed | tf_op | source)
XLA Modules:
  0.0 223.8 jit_solution(18237244186164771223)
XLA Ops:
  6.5 0.0 all-gather.2.cloned.1.call-start
  6.5 0.7 convert_element_type.15
  7.3 0.1 fusion.34
  7.4 0.1 sin.8
  7.5 1.9 fusion.13
  9.5 1.4 pad_maximum_fusion
  10.9 0.0 all-gather.2.cloned.1.call-update
  10.9 0.0 reduce-scatter.2.cloned.1.call-start
  10.9 131.4 %all-gather.2.cloned.1.call-done = bf16[2,16384,384]{2,1,0:T(8,128)(2,1)} async-done(((bf16[2,1024,384]{2,1,0:T(8,128)(2,1)}), bf16[2,16384,384]{2,1,0:T(8,128)(2,1)}) %all-gather.2.cloned.1.call-update) | async-done | bytes 25165840 | tf_op jit(solution)/shard_map/all_gather | solution.py:27
  142.3 13.9 %fusion = f32[384,512]{1,0:T(8,128)S(1)} fusion(bf16[2,512,16384]{2,1,0:T(8,128)(2,1)} %param.3, bf16[2,16384,384]{2,1,0:T(8,128)(2,1)} %all-gather.2.cloned.1.call-done), kind=kOutput, calls=%fused_computation | convolution fusion | flops 6442450944 | bytes 30146560 | tf_op jit(solution)/shard_map/dot_general | solution.py:33
  156.2 14.0 %fusion.2 = f32[384,512]{1,0:T(8,128)S(1)} fusion(bf16[2,512,16384]{2,1,0:T(8,128)(2,1)} %param.3, bf16[2,16384,384]{2,1,0:T(8,128)(2,1)} %all-gather.2.cloned.1.call-done), kind=kOutput, calls=%fused_computation.2 | convolution fusion | flops 6442450944 | bytes 30146560 | tf_op jit(solution)/shard_map/dot_general | solution.py:30
  170.2 14.0 %fusion.31 = bf16[1,512,384]{1,2,0:T(8,128)(2,1)S(1)} fusion(f32[384,512]{1,0:T(8,128)S(1)} %fusion, bf16[2,512,16384]{2,1,0:T(8,128)(2,1)} %param.3, bf16[2,16384,384]{2,1,0:T(8,128)(2,1)} %all-gather.2.cloned.1.call-done), kind=kOutput, calls=%fused_computation.28 | convolution fusion | flops 6442844160 | bytes 30539776 | tf_op jit(solution)/shard_map/dot_general | solution.py:33
  184.2 14.1 %fusion.28 = bf16[1,512,384]{1,2,0:T(8,128)(2,1)S(1)} fusion(f32[384,512]{1,0:T(8,128)S(1)} %fusion.2, bf16[2,512,16384]{2,1,0:T(8,128)(2,1)} %param.3, bf16[2,16384,384]{2,1,0:T(8,128)(2,1)} %all-gather.2.cloned.1.call-done), kind=kOutput, calls=%fused_computation.27 | convolution fusion | flops 6442844160 | bytes 30539776 | tf_op jit(solution)/shard_map/dot_general | solution.py:30
  198.3 1.0 pad_maximum_fusion.1
  199.3 0.0 reduce-scatter.2.cloned.1.call-update
  199.3 17.6 %reduce-scatter.2.cloned.1.call-done = bf16[2,512,192]{1,2,0:T(8,128)(2,1)} async-done(((bf16[2,512,384]{1,2,0:T(8,128)(2,1)}), bf16[2,512,192]{1,2,0:T(8,128)(2,1)}) %reduce-scatter.2.cloned.1.call-update) | async-done | bytes 393232 | tf_op jit(solution)/shard_map/reduce_scatter | solution.py:37
Async XLA Ops:
  6.5 135.8 %all-gather.2.cloned.1.call-start = ((), (), s32[]{:S(2)}) async-start(), calls=%async_computation.1 | async-start | bytes 26738688 | tf_op jit(solution)/shard_map/all_gather | solution.py:27
  10.9 206.0 %reduce-scatter.2.cloned.1.call-start = ((), (), s32[]{:S(2)}) async-start(), calls=%async_computation.2 | async-start | bytes 1179648 | tf_op jit(solution)/shard_map/reduce_scatter | solution.py:37
Sparse Core Ops, SparseCore 0:
  11.0 131.2 all-gather.1
  199.4 17.4 reduce-scatter.1
where the time goes:
time: 224 us
  waiting for transfers between devices  149 us (67%)
  matrix products  56 us (25%)
  between operations  13.4 us (6%)
  other arithmetic  5.15 us (2%)
    all_gather x1, waiting for transfers between devices, per_device(): gathered = lax.all_gather(phased, 'row', axis=1, tiled=True)  131 us
    reduce_scatter x1, waiting for transfers between devices, per_device(): lax.psum_scatter(totals.astype(jnp.bfloat16), 'col', scatter_dimension=2,...  17.6 us
    dot_general x1, matrix products, per_device(): jnp.dot(s_real, gathered[0], preferred_element_type=jnp.float32)  14.1 us
    dot_general x1, matrix products, per_device(): jnp.dot(s_imag, gathered[1], preferred_element_type=jnp.float32)  14 us
    dot_general x1, matrix products, per_device(): jnp.dot(s_real, gathered[1], preferred_element_type=jnp.float32)  14 us
    dot_general x1, matrix products, per_device(): jnp.dot(s_imag, gathered[0], preferred_element_type=jnp.float32)  13.9 us
  transfers between devices with their start and end apart: 2, of which 2 were waited for; matrix products, arithmetic and copies ran while one was open for 0% of the time, Pallas kernels for 0%

commit v1 on v0

v1 whole, which is shorter than its diff:
```python
import jax
import jax.numpy as jnp
import numpy as np
from jax import lax
from jax.experimental import pallas as pl
from jax.experimental.pallas import tpu as pltpu
from jax.sharding import PartitionSpec as P

PER_PLANE = 4
SLOTS = 4
IN_VMEM = pl.BlockSpec(memory_space=pltpu.VMEM)


def angles_of(hkl):
    h, k, l = (hkl[i : i + 1].astype(jnp.float32) for i in range(3))
    return 0.61 * (h * h + k * k + l * l) + 0.29 * h - 0.17 * k + 0.43 * l


def apply_phase(slab, beam_hkl):
    angles = angles_of(beam_hkl)
    cosine, sine = jnp.cos(angles), jnp.sin(angles)
    turned = jnp.swapaxes(slab, 1, 2).astype(jnp.float32)
    phased_real = cosine * turned[0] - sine * turned[1]
    phased_imag = cosine * turned[1] + sine * turned[0]
    return phased_real.astype(jnp.bfloat16), phased_imag.astype(jnp.bfloat16)


def phase_panels(slab, beam_hkl):
    _, depth, columns = slab.shape
    w = columns // 2

    def kernel(slab_ref, hkl_ref, whole_ref, first_ref, second_ref):
        col = lax.axis_index("col")
        angles = angles_of(hkl_ref[...])
        cosine, sine = jnp.cos(angles), jnp.sin(angles)
        row = lax.broadcasted_iota(jnp.int32, (columns, columns), 0)
        lane = lax.broadcasted_iota(jnp.int32, (columns, columns), 1)
        wanted = jnp.where(col == 0, jnp.where(row < w, row + w, row - w), row)
        select = jnp.where(lane == wanted, 1.0, 0.0).astype(jnp.bfloat16)

        def turned(part):
            return lax.dot_general(
                select, slab_ref[part], (((1,), (1,)), ((), ())), preferred_element_type=jnp.float32
            )

        real, imag = turned(0), turned(1)
        phased_real = (cosine * real - sine * imag).astype(jnp.bfloat16)
        phased_imag = (cosine * imag + sine * real).astype(jnp.bfloat16)
        for k, half_ref in enumerate((first_ref, second_ref)):
            rows = slice(k * w, (k + 1) * w)
            for j, phased in enumerate((phased_real, phased_imag)):
                half_ref[j * w : (j + 1) * w, :] = phased[rows]
                whole_ref[(2 * k + j) * w : (2 * k + j + 1) * w, :] = phased[rows]

    return pl.pallas_call(
        kernel,
        out_shape=[jax.ShapeDtypeStruct((n * columns, depth), jnp.bfloat16) for n in (2, 1, 1)],
        out_specs=[IN_VMEM] * 3,
        compiler_params=pltpu.CompilerParams(vmem_limit_bytes=34 * 2**20),
        cost_estimate=pl.CostEstimate(flops=1000, bytes_accessed=1000, transcendentals=0),
    )(slab, beam_hkl)


def after(value, *others):
    return lax.optimization_barrier((value,) + others)[0]


def multiply(which, blocks, s_matrix, pieces, total=None, finish=False, received=None):
    count = len(pieces)
    spans = [p[1:] if isinstance(p, tuple) else (0, p.shape[0]) for p in pieces]
    pieces = [p[0] if isinstance(p, tuple) else p for p in pieces]
    total_from = total[1] if isinstance(total, tuple) else 0
    in_place = total is not None and not isinstance(total, tuple) and not finish
    total = total[0] if isinstance(total, tuple) else total
    width, depth = spans[0][1], pieces[0].shape[1]
    rows = s_matrix.shape[1]
    half = width // 2
    extra = [v for v in (total, received) if v is not None]
    jobs = [(p, part) for p in range(count) for part in range(2)]
    slots = min(SLOTS, len(jobs))

    def kernel(blocks_ref, s_ref, *refs):
        piece_refs = refs[:count]
        total_ref = refs[count] if total is not None else None
        received_ref = refs[count + len(extra) - 1] if received is not None else None
        out_ref, held, arrived = refs[count + len(extra) : count + len(extra) + 3]
        sum_ref = refs[-1] if finish else out_ref

        def fetch(n):
            p, part = jobs[n]
            start = pl.multiple_of(blocks_ref[which[p]] * depth, depth)
            return pltpu.make_async_copy(
                s_ref.at[part, :, pl.ds(start, depth)], held.at[n % slots], arrived.at[n % slots]
            )

        for n in range(slots):
            fetch(n).start()
        for n, (p, part) in enumerate(jobs):
            fetch(n).wait()
            lanes = slice(part * rows, (part + 1) * rows)
            piece = piece_refs[p][spans[p][0] : spans[p][0] + width, :]
            product = lax.dot_general(
                piece, held[n % slots], (((1,), (1,)), ((), ())), preferred_element_type=jnp.float32
            )
            if p > 0:
                sum_ref[:, lanes] += product
            elif total is None:
                sum_ref[:, lanes] = product
            else:
                sum_ref[:, lanes] = total_ref[total_from : total_from + width, lanes] + product
            if n + slots < len(jobs):
                fetch(n + slots).start()
        if finish:
            real = sum_ref[:half, :rows] - sum_ref[half:, rows:]
            imag = sum_ref[half:, :rows] + sum_ref[:half, rows:]
            if received is not None:
                real += received_ref[0].astype(jnp.float32)
                imag += received_ref[1].astype(jnp.float32)
            out_ref[0] = real.astype(out_ref.dtype)
            out_ref[1] = imag.astype(out_ref.dtype)

    scratch = [pltpu.VMEM((slots, rows, depth), s_matrix.dtype), pltpu.SemaphoreType.DMA((slots,))]
    if finish:
        out_shape = jax.ShapeDtypeStruct((2, half, rows), jnp.bfloat16)
        scratch.append(pltpu.VMEM((width, 2 * rows), jnp.float32))
    else:
        out_shape = jax.ShapeDtypeStruct((width, 2 * rows), jnp.float32)
    return pl.pallas_call(
        kernel,
        out_shape=out_shape,
        in_specs=[pl.BlockSpec(memory_space=pltpu.SMEM), pl.BlockSpec(memory_space=pltpu.HBM)]
        + [IN_VMEM] * (count + len(extra)),
        out_specs=IN_VMEM,
        scratch_shapes=scratch,
        input_output_aliases={2 + count: 0} if in_place else {},
        compiler_params=pltpu.CompilerParams(vmem_limit_bytes=34 * 2**20),
        cost_estimate=pl.CostEstimate(flops=1000, bytes_accessed=1000, transcendentals=0),
    )(blocks, s_matrix, *pieces, *extra)


def choose(flag, first, second, row=0):
    rows = second.shape[0]

    def kernel(flag_ref, first_ref, second_ref, out_ref, done):
        del second_ref

        @pl.when(flag_ref[0] == 1)
        def _():
            copy = pltpu.make_async_copy(first_ref.at[row : row + rows, :], out_ref, done)
            copy.start()
            copy.wait()

    return pl.pallas_call(
        kernel,
        out_shape=jax.ShapeDtypeStruct(second.shape, second.dtype),
        in_specs=[pl.BlockSpec(memory_space=pltpu.SMEM)] + [pl.BlockSpec(memory_space=pl.ANY)] * 2,
        out_specs=pl.BlockSpec(memory_space=pl.ANY),
        scratch_shapes=[pltpu.SemaphoreType.DMA],
        input_output_aliases={2: 0},
        compiler_params=pltpu.CompilerParams(vmem_limit_bytes=34 * 2**20),
        cost_estimate=pl.CostEstimate(flops=1000, bytes_accessed=1000, transcendentals=0),
    )(flag, first, second)


def line_of_four(s_matrix, slab, beam_hkl):
    n_row = lax.axis_size("row")
    every = [(z, x, c) for z in range(n_row // PER_PLANE) for x in range(2) for c in range(2)]

    def index(z, x, c):
        return (z * 2 + x) * 2 + c

    def pairs(target, planes=(0, 1, 2, 3)):
        return [(index(*at), index(*target(*at))) for at in every if at[0] in planes]

    across = pairs(lambda z, x, c: (z, 1 - x, c))
    sibling = pairs(lambda z, x, c: (z, x, 1 - c))
    outer = pairs(lambda z, x, c: (z ^ 1, x, c))
    middle = pairs(lambda z, x, c: (3 - z, x, c), (1, 2))
    outward = pairs(lambda z, x, c: (z ^ 1, x, c), (1, 2))

    def send(value, route, what):
        with jax.named_scope("L_" + what):
            return lax.ppermute(value, "row", route)

    def far1(z):
        return 3 - z if z in (1, 2) else z ^ 2

    def far2(z):
        return z ^ 2 if z in (1, 2) else 3 - z

    me = lax.axis_index("row")
    held = {"O": lambda z: z, "P": lambda z: z ^ 1, "M": far1, "N": far2}
    names = [x + c + o for x in ("", "x") for c in ("", "c") for o in held]
    table = [
        [index(held[n[-1]](z), 1 - x if "x" in n else x, 1 - c if "c" in n else c) for n in names]
        + [int(z in (1, 2))]
        for z, x, c in every
    ]
    here = jnp.asarray(np.array(table, np.int32))[me]

    in_middle = here[len(names) :]
    O, Oa, Ob = phase_panels(slab, beam_hkl)
    wide = Oa.shape[0]

    def a(v):
        return (v, 0, wide)

    def b(v):
        return (v, wide, wide)

    def X(v, n):
        return send(v, across, "X" + n)

    def C(v, n):
        return send(v, sibling, "C" + n)

    def mul(which, pieces, total, **kw):
        return multiply([names.index(n) for n in which], here, s_matrix, pieces, total, **kw)

    ob = lax.optimization_barrier
    XO, P, Qa, Qb = X(O, "O"), send(O, outer, "P"), send(Oa, middle, "Qa"), send(Ob, middle, "Qb")
    CO = C(O, "O")
    AB = mul(["O", "cO"], [O, CO], None)
    Sa = send(Qa, outward, "Sa")
    P, Qb, XO, AB = ob((P, Qb, XO, AB))
    XPa, Sb, T = X(P[:wide], "Pa"), send(Qb, outward, "Sb"), send(P, middle, "T")
    CP, CXO = C(P, "P"), C(XO, "XO")
    AB = mul(["P", "xO"], [P, XO], AB)
    XPa, Sa, AB = ob((XPa, Sa, AB))
    M1a = choose(in_middle, Qa, Sa)
    XM1a = X(M1a, "M1a")
    CXPa, CM1a = C(XPa, "XPa"), C(M1a, "M1a")
    AB = mul(["cP", "xcO"], [CP, CXO], AB)
    A = mul(["xP", "M"], [XPa, M1a], a(AB))
    XM1a, T, Sb, A, AB = ob((XM1a, T, Sb, A, AB))
    M1b = choose(in_middle, Qb, Sb)
    XM1b = X(M1b, "M1b")
    Ua, Ub = send(T[:wide], outward, "Ua"), send(T[wide:], outward, "Ub")
    CXM1a, CM1b = C(XM1a, "XM1a"), C(M1b, "M1b")
    A = mul(["xcP", "cM", "xM"], [CXPa, CM1a, XM1a], A)
    XM1b, Ua, A = ob((XM1b, Ua, A))
    M2a = choose(in_middle, T, Ua)
    XM2a = X(M2a, "M2a")
    E = send(after(XO, Ua)[wide:], outer, "E")
    CXM1b, CM2a = C(XM1b, "XM1b"), C(M2a, "M2a")
    B = mul(["M", "cM", "xM"], [M1b, CM1b, XM1b], b(AB))
    A = mul(["N", "xcM"], [M2a, CXM1a], A)
    XM2a, Ub, A, B = ob((XM2a, Ub, A, B))
    M2b = choose(in_middle, T, Ub, wide)
    XM2b = X(M2b, "M2b")
    CXM2a, CM2b = C(XM2a, "XM2a"), C(M2b, "M2b")
    partial = mul(["cN", "xN", "xcN"], [CM2a, XM2a, CXM2a], A, finish=True)
    with jax.named_scope("L_partial"):
        received = lax.ppermute(partial, "col", [(0, 1), (1, 0)])
    B = mul(["xcM", "N"], [CXM1b, M2b], B)
    XM2b, E, B, received = ob((XM2b, E, B, received))
    CXM2b, CE = C(XM2b, "XM2b"), C(E, "E")
    B = mul(["cN", "xN", "xP"], [CM2b, XM2b, E], B)
    out = mul(["xcN", "xcP"], [CXM2b, CE], B, finish=True, received=received)
    return jnp.swapaxes(out, 1, 2)


def any_mesh(s_matrix, slab, beam_hkl):
    real, imag = apply_phase(slab, beam_hkl)
    gathered = lax.all_gather(jnp.stack([real, imag]), "row", axis=2, tiled=True)

    def dot(s, x):
        return lax.dot_general(x, s, (((1,), (1,)), ((), ())), preferred_element_type=jnp.float32)

    part_real = dot(s_matrix[0], gathered[0]) - dot(s_matrix[1], gathered[1])
    part_imag = dot(s_matrix[0], gathered[1]) + dot(s_matrix[1], gathered[0])
    totals = jnp.stack([part_real, part_imag]).astype(jnp.bfloat16)
    return jnp.swapaxes(lax.psum_scatter(totals, "col", scatter_dimension=1, tiled=True), 1, 2)


def solution(mesh):
    placed = (P(None, "row", "col"), P(None, ("col", "row"), None), P(None, ("col", "row")))
    line = mesh.shape["row"] == 4 * PER_PLANE and mesh.shape["col"] == 2
    return jax.shard_map(
        line_of_four if line else any_mesh,
        mesh=mesh,
        in_specs=placed,
        out_specs=P(None, "row", "col"),
        check_vma=False,
    )
```

time: 224 us -> 162 us (0.72)
  waiting for transfers between devices: 149 us -> 68.1 us
  Pallas kernels: 0 us -> 62.9 us
  matrix products: 56 us -> 0 us
  starting transfers between devices: 0.04 us -> 26.5 us
  between operations: 13.4 us -> 0.42 us
  other arithmetic: 5.15 us -> 0 us
  local copies, waits for them, and re-layouts: 0.12 us -> 3.62 us
    all_gather x1 -> x0, waiting for transfers between devices: 131 us -> none  [per_device(): gathered = lax.all_gather(phased, 'row', axis=1, tiled=True)]
    ppermute x0 -> x29, waiting for transfers between devices: none -> 68.1 us  [the longest x28 68.1 us: send(): return lax.ppermute(value, 'row', route)]
    pallas_call x0 -> x16, Pallas kernels: none -> 62.9 us  [the longest x11 57.3 us: multiply(): pl.pallas_call(kernel, out_shape=out_shape, in_specs=[pl.BlockSpec(memory...]
    dot_general x4 -> x0, matrix products: 56 us -> none  [the longest x1 14.1 us: per_device(): jnp.dot(s_real, gathered[0], preferred_element_type=jnp.float32)]
    ppermute x0 -> x29, starting transfers between devices: none -> 26.5 us  [the longest x28 24.9 us: send(): return lax.ppermute(value, 'row', route)]
    reduce_scatter x1 -> x0, waiting for transfers between devices: 17.6 us -> none  [per_device(): lax.psum_scatter(totals.astype(jnp.bfloat16), 'col', scatter_dimension=2,...]
    another operation x3 -> x0, other arithmetic: 4.29 us -> none
  transfers between devices with their start and end apart: 2 -> 29, of which waited for: 2 -> 10; matrix products, arithmetic and copies ran while one was open for 0% -> 1% of each run, Pallas kernels for 0% -> 34%
where the time goes in v1:
time: 162 us
  waiting for transfers between devices  68.1 us (42%)
  Pallas kernels  62.9 us (39%)
  starting transfers between devices  26.5 us (16%)
  local copies, waits for them, and re-layouts  3.62 us (2%)
    ppermute x28, waiting for transfers between devices, send(): return lax.ppermute(value, 'row', route)  68.1 us
    pallas_call x11, Pallas kernels, multiply(): pl.pallas_call(kernel, out_shape=out_shape, in_specs=[pl.BlockSpec(memory...  57.3 us
    ppermute x28, starting transfers between devices, send(): return lax.ppermute(value, 'row', route)  24.9 us
  transfers between devices with their start and end apart: 29, of which 10 were waited for; matrix products, arithmetic and copies ran while one was open for 1% of the time, Pallas kernels for 34%

profile of v1, /device:TPU:0, one launch (start us, length us, event | category | flops | bytes accessed | tf_op | source)
XLA Modules:
  0.0 161.6 jit_solution(14291013762055426046)
XLA Ops:
  0.0 1.4 copy-done
  1.4 0.7 copy-done.1
  2.1 2.8 %shard_map.46 = (bf16[768,1024]{1,0:T(8,128)(2,1)}, bf16[384,1024]{1,0:T(8,128)(2,1)}, bf16[384,1024]{1,0:T(8,128)(2,1)}) custom-call(bf16[2,1024,384]{2,1,0:T(8,128)(2,1)S(1)} %copy-done, s32[3,1024]{1,0:T(4,128)S(1)} %copy-done.1), custom_call_target="tpu_custom_call" | custom-call | flops 1000 | bytes 1000 | tf_op jit(solution)/shard_map/pallas_call | solution.py:55
  5.3 2.6 %collective-permute-start.1 = (bf16[768,1024]{1,0:T(8,128)(2,1)}, bf16[768,1024]{1,0:T(8,128)(2,1)S(1)}, u32[]{:S(2)}, u32[]{:S(2)}) collective-permute-start(bf16[768,1024]{1,0:T(8,128)(2,1)} %get-tuple-element.33.refs_0_), channel_id=1, source_target_pairs={{0,8},{2,10},{4,12},{6,14},{8,0},{10,2},{12,4},{14,6},{16,24},{18,... | collective-permute-start | bytes 4718600 | tf_op jit(solution)/shard_map/L_P/ppermute | solution.py:183
  7.9 1.5 collective-permute-start.3
  9.4 1.6 collective-permute-start
  11.0 1.6 collective-permute-start.2
  12.5 0.7 constant_dynamic-slice_fusion
  13.2 1.3 collective-permute-start.6
  14.5 7.2 %shard_map.47.refs_2_ = f32[768,1024]{1,0:T(8,128)S(1)} custom-call(s32[17]{0:T(128)S(1)} %get-tuple-element.62.blocks_ref, bf16[2,512,16384]{2,1,0:T(8,128)(2,1)} %s_ref.21, bf16[768,1024]{1,0:T(8,128)(2,1)} %get-tuple-element.33.refs_0_, bf16[768,1024]{1,0:T(8,128)(2,1)} %collective-permute-done.4.refs_1_), custom_call_target="tpu_custom_call" | custom-call | flops 1000 | bytes 1000 | tf_op jit(solution)/shard_map/pallas_call | solution.py:128
  21.8 21.6 %collective-permute-done.1.refs_0_ = bf16[768,1024]{1,0:T(8,128)(2,1)S(1)} collective-permute-done((bf16[768,1024]{1,0:T(8,128)(2,1)}, bf16[768,1024]{1,0:T(8,128)(2,1)S(1)}, u32[]{:S(2)}, u32[]{:S(2)}) %collective-permute-start.1) | collective-permute-done | bytes 1572896 | tf_op jit(solution)/shard_map/L_P/ppermute | solution.py:183
  43.4 1.3 collective-permute-done.3.refs_1_
  45.3 1.5 collective-permute-start.5
  46.8 0.7 collective-permute-start.8
  47.5 0.6 slice.18
  48.1 6.0 %shard_map.48.refs_2_ = f32[768,1024]{1,0:T(8,128)S(1)} custom-call(s32[17]{0:T(128)S(1)} %get-tuple-element.62.blocks_ref, bf16[2,512,16384]{2,1,0:T(8,128)(2,1)} %s_ref.21, bf16[768,1024]{1,0:T(8,128)(2,1)S(1)} %collective-permute-done.1.refs_0_, bf16[768,1024]{1,0:T(8,128)(2,1)S(1)} %collective-permute-done.3.refs_1_, ...), custom_call_target="tpu_custom_call", output_to_operand_aliasing={{}: (4, {})} | custom-call | flops 1000 | bytes 1000 | tf_op jit(solution)/shard_map/pallas_call | solution.py:128
  54.1 5.9 %collective-permute-done.6.second_ref = bf16[384,1024]{1,0:T(8,128)(2,1)S(1)} collective-permute-done((bf16[384,1024]{1,0:T(8,128)(2,1)}, bf16[384,1024]{1,0:T(8,128)(2,1)S(1)}, u32[]{:S(2)}, u32[]{:S(2)}) %collective-permute-start.6) | collective-permute-done | bytes 786464 | tf_op jit(solution)/shard_map/L_Sa/ppermute | solution.py:183
  60.0 1.5 collective-permute-start.9
  61.5 3.3 %collective-permute-done.5.refs_0_ = bf16[384,1024]{1,0:T(8,128)(2,1)S(1)} collective-permute-done((bf16[384,1024]{1,0:T(8,128)(2,1)S(1)}, bf16[384,1024]{1,0:T(8,128)(2,1)S(1)}, u32[]{:S(2)}, u32[]{:S(2)}) %collective-permute-start.5) | collective-permute-done | bytes 786464 | tf_op jit(solution)/shard_map/L_XPa/ppermute | solution.py:183
  64.8 0.7 shard_map.49.refs_1_
  65.5 1.6 collective-permute-start.7
  67.0 6.0 %shard_map.50.refs_2_.refs_3_ = f32[768,1024]{1,0:T(8,128)S(1)} custom-call(s32[17]{0:T(128)S(1)} %get-tuple-element.62.blocks_ref, bf16[2,512,16384]{2,1,0:T(8,128)(2,1)} %s_ref.21, bf16[768,1024]{1,0:T(8,128)(2,1)S(1)} %collective-permute-done.10.refs_0_, bf16[768,1024]{1,0:T(8,128)(2,1)S(1)} %collective-permute-done.11.refs_1_, ...), custom_call_target="tpu_custom_call", output_to_operand_aliasing={{}: (4, {})} | custom-call | flops 1000 | bytes 1000 | tf_op jit(solution)/shard_map/pallas_call | solution.py:128
  73.1 0.6 collective-permute-start.14
  73.7 4.1 %shard_map.51.refs_3_ = f32[384,1024]{1,0:T(8,128)S(1)} custom-call(s32[17]{0:T(128)S(1)} %get-tuple-element.62.blocks_ref, bf16[2,512,16384]{2,1,0:T(8,128)(2,1)} %s_ref.21, bf16[384,1024]{1,0:T(8,128)(2,1)S(1)} %collective-permute-done.5.refs_0_, bf16[384,1024]{1,0:T(8,128)(2,1)S(1)} %shard_map.49.refs_1_, f32[768,1024]{1,0:T(8,128)S(1)} %shard_map.50.refs_2_.refs_3_), custom_call_target="tpu_custom_call" | custom-call | flops 1000 | bytes 1000 | tf_op jit(solution)/shard_map/pallas_call | solution.py:128
  77.8 3.7 %collective-permute-done.9.second_ref = bf16[384,1024]{1,0:T(8,128)(2,1)S(1)} collective-permute-done((bf16[384,1024]{1,0:T(8,128)(2,1)}, bf16[384,1024]{1,0:T(8,128)(2,1)S(1)}, u32[]{:S(2)}, u32[]{:S(2)}) %collective-permute-start.9) | collective-permute-done | bytes 786464 | tf_op jit(solution)/shard_map/L_Sb/ppermute | solution.py:183
  81.5 2.7 %collective-permute-done.7.refs_2_ = bf16[384,1024]{1,0:T(8,128)(2,1)S(1)} collective-permute-done((bf16[384,1024]{1,0:T(8,128)(2,1)S(1)}, bf16[384,1024]{1,0:T(8,128)(2,1)S(1)}, u32[]{:S(2)}, u32[]{:S(2)}) %collective-permute-start.7) | collective-permute-done | bytes 786464 | tf_op jit(solution)/shard_map/L_XM1a/ppermute | solution.py:183
  84.3 1.3 collective-permute-start.13
  85.6 0.7 shard_map.52.refs_0_
  86.3 1.6 collective-permute-start.12
  88.4 5.2 %shard_map.53.refs_2_ = f32[384,1024]{1,0:T(8,128)S(1)} custom-call(s32[17]{0:T(128)S(1)} %get-tuple-element.62.blocks_ref, bf16[2,512,16384]{2,1,0:T(8,128)(2,1)} %s_ref.21, bf16[384,1024]{1,0:T(8,128)(2,1)S(1)} %collective-permute-done.14.refs_0_, bf16[384,1024]{1,0:T(8,128)(2,1)S(1)} %collective-permute-done.15.refs_1_, ...), custom_call_target="tpu_custom_call", output_to_operand_aliasing={{}: (5, {})} | custom-call | flops 1000 | bytes 1000 | tf_op jit(solution)/shard_map/pallas_call | solution.py:128
  93.6 13.8 %collective-permute-done.13.second_ref = bf16[384,1024]{1,0:T(8,128)(2,1)S(1)} collective-permute-done((bf16[384,1024]{1,0:T(8,128)(2,1)S(1)}, bf16[384,1024]{1,0:T(8,128)(2,1)S(1)}, u32[]{:S(2)}, u32[]{:S(2)}) %collective-permute-start.13) | collective-permute-done | bytes 786464 | tf_op jit(solution)/shard_map/L_Ua/ppermute | solution.py:183
  107.4 1.3 collective-permute-start.17
  108.7 0.7 shard_map.54.refs_0_
  109.4 0.6 collective-permute-start.16
  110.0 4.2 %shard_map.55.refs_3_ = f32[384,1024]{1,0:T(8,128)S(1)} custom-call(s32[17]{0:T(128)S(1)} %get-tuple-element.62.blocks_ref, bf16[2,512,16384]{2,1,0:T(8,128)(2,1)} %s_ref.21, bf16[384,1024]{1,0:T(8,128)(2,1)S(1)} %shard_map.54.refs_0_, bf16[384,1024]{1,0:T(8,128)(2,1)S(1)} %collective-permute-done.18.refs_1_, ...), custom_call_target="tpu_custom_call", output_to_operand_aliasing={{}: (4, {})} | custom-call | flops 1000 | bytes 1000 | tf_op jit(solution)/shard_map/pallas_call | solution.py:128
  114.2 5.1 %shard_map.56.refs_2_ = f32[384,1024]{1,0:T(8,128)S(1)} custom-call(s32[17]{0:T(128)S(1)} %get-tuple-element.62.blocks_ref, bf16[2,512,16384]{2,1,0:T(8,128)(2,1)} %s_ref.21, bf16[384,1024]{1,0:T(8,128)(2,1)S(1)} %shard_map.52.refs_0_, bf16[384,1024]{1,0:T(8,128)(2,1)S(1)} %collective-permute-done.19.refs_1_, ...), custom_call_target="tpu_custom_call" | custom-call | flops 1000 | bytes 1000 | tf_op jit(solution)/shard_map/pallas_call | solution.py:128
  119.4 8.1 %collective-permute-done.17.second_ref = bf16[384,1024]{1,0:T(8,128)(2,1)S(1)} collective-permute-done((bf16[384,1024]{1,0:T(8,128)(2,1)S(1)}, bf16[384,1024]{1,0:T(8,128)(2,1)S(1)}, u32[]{:S(2)}, u32[]{:S(2)}) %collective-permute-start.17) | collective-permute-done | bytes 786464 | tf_op jit(solution)/shard_map/L_Ub/ppermute | solution.py:183
  127.4 0.5 collective-permute-start.22
  128.0 2.7 %collective-permute-start.21 = (bf16[384,1024]{1,0:T(8,128)(2,1)S(1)}, bf16[384,1024]{1,0:T(8,128)(2,1)S(1)}, u32[]{:S(2)}, u32[]{:S(2)}) collective-permute-start(bf16[384,1024]{1,0:T(8,128)(2,1)S(1)} %slice.23), channel_id=1, source_target_pairs={{0,8},{2,10},{4,12},{6,14},{8,0},{10,2},{12,4},{14,6},{16,24},{18,... | collective-permute-start | bytes 2359304 | tf_op jit(solution)/shard_map/L_E/ppermute | solution.py:183
  130.7 0.9 shard_map.57.refs_1_
  131.6 0.6 collective-permute-start.20
  132.2 5.1 %shard_map.59 = bf16[2,192,512]{2,1,0:T(8,128)(2,1)S(1)} custom-call(s32[17]{0:T(128)S(1)} %get-tuple-element.62.blocks_ref, bf16[2,512,16384]{2,1,0:T(8,128)(2,1)} %s_ref.21, bf16[384,1024]{1,0:T(8,128)(2,1)S(1)} %collective-permute-done.23.refs_0_, bf16[384,1024]{1,0:T(8,128)(2,1)S(1)} %collective-permute-done.16.refs_1_, ...), custom_call_target="tpu_custom_call" | custom-call | flops 1000 | bytes 1000 | tf_op jit(solution)/shard_map/pallas_call | solution.py:128
  137.2 1.6 collective-permute-start.25
  138.8 4.2 %shard_map.58.refs_3_ = f32[384,1024]{1,0:T(8,128)S(1)} custom-call(s32[17]{0:T(128)S(1)} %get-tuple-element.62.blocks_ref, bf16[2,512,16384]{2,1,0:T(8,128)(2,1)} %s_ref.21, bf16[384,1024]{1,0:T(8,128)(2,1)S(1)} %collective-permute-done.22.refs_0_, bf16[384,1024]{1,0:T(8,128)(2,1)S(1)} %shard_map.57.refs_1_, ...), custom_call_target="tpu_custom_call", output_to_operand_aliasing={{}: (4, {})} | custom-call | flops 1000 | bytes 1000 | tf_op jit(solution)/shard_map/pallas_call | solution.py:128
  143.1 5.3 %collective-permute-done.21.refs_2_ = bf16[384,1024]{1,0:T(8,128)(2,1)S(1)} collective-permute-done((bf16[384,1024]{1,0:T(8,128)(2,1)S(1)}, bf16[384,1024]{1,0:T(8,128)(2,1)S(1)}, u32[]{:S(2)}, u32[]{:S(2)}) %collective-permute-start.21) | collective-permute-done | bytes 786464 | tf_op jit(solution)/shard_map/L_E/ppermute | solution.py:183
  148.4 2.4 %collective-permute-done.20.refs_1_ = bf16[384,1024]{1,0:T(8,128)(2,1)S(1)} collective-permute-done((bf16[384,1024]{1,0:T(8,128)(2,1)S(1)}, bf16[384,1024]{1,0:T(8,128)(2,1)S(1)}, u32[]{:S(2)}, u32[]{:S(2)}) %collective-permute-start.20) | collective-permute-done | bytes 786464 | tf_op jit(solution)/shard_map/L_XM2b/ppermute | solution.py:183
  151.3 5.2 %shard_map.60.refs_2_ = f32[384,1024]{1,0:T(8,128)S(1)} custom-call(s32[17]{0:T(128)S(1)} %get-tuple-element.62.blocks_ref, bf16[2,512,16384]{2,1,0:T(8,128)(2,1)} %s_ref.21, bf16[384,1024]{1,0:T(8,128)(2,1)S(1)} %collective-permute-done.28.refs_0_, bf16[384,1024]{1,0:T(8,128)(2,1)S(1)} %collective-permute-done.20.refs_1_, ...), custom_call_target="tpu_custom_call", output_to_operand_aliasing={{}: (5, {})} | custom-call | flops 1000 | bytes 1000 | tf_op jit(solution)/shard_map/pallas_call | solution.py:128
  156.6 4.9 %shard_map.61 = bf16[2,192,512]{2,1,0:T(8,128)(2,1)} custom-call(s32[17]{0:T(128)S(1)} %get-tuple-element.62.blocks_ref, bf16[2,512,16384]{2,1,0:T(8,128)(2,1)} %s_ref.21, bf16[384,1024]{1,0:T(8,128)(2,1)S(1)} %collective-permute-done.26.refs_0_, bf16[384,1024]{1,0:T(8,128)(2,1)S(1)} %collective-permute-done.27.refs_1_, f32[384,1024]{1,0:T(8,128)S(1)} %shard_map.60.refs_2_, ...), custom_call_target="tpu_custom_call" | custom-call | flops 1000 | bytes 1000 | tf_op jit(solution)/shard_map/pallas_call | solution.py:128
  (35 shorter events, 2.3 us)
Async XLA Ops:
  0.0 1.4 copy-start
  1.4 0.7 copy-start.1
  4.9 9.6 %collective-permute-start.4 = (bf16[768,1024]{1,0:T(8,128)(2,1)}, bf16[768,1024]{1,0:T(8,128)(2,1)}, u32[]{:S(2)}, u32[]{:S(2)}) collective-permute-start(bf16[768,1024]{1,0:T(8,128)(2,1)} %get-tuple-element.33.refs_0_), channel_id=1, source_target_pairs={{0,2},{2,0},{4,6},{6,4},{8,10},{10,8},{12,14},{14,12},{16,18},{18,... | collective-permute-start | bytes 4718600 | tf_op jit(solution)/shard_map/L_CO/ppermute | solution.py:183
  5.3 38.0 %collective-permute-start.1 = (bf16[768,1024]{1,0:T(8,128)(2,1)}, bf16[768,1024]{1,0:T(8,128)(2,1)S(1)}, u32[]{:S(2)}, u32[]{:S(2)}) collective-permute-start(bf16[768,1024]{1,0:T(8,128)(2,1)} %get-tuple-element.33.refs_0_), channel_id=1, source_target_pairs={{0,8},{2,10},{4,12},{6,14},{8,0},{10,2},{12,4},{14,6},{16,24},{18,... | collective-permute-start | bytes 4718600 | tf_op jit(solution)/shard_map/L_P/ppermute | solution.py:183
  7.9 36.7 %collective-permute-start.3 = (bf16[768,1024]{1,0:T(8,128)(2,1)}, bf16[768,1024]{1,0:T(8,128)(2,1)S(1)}, u32[]{:S(2)}, u32[]{:S(2)}) collective-permute-start(bf16[768,1024]{1,0:T(8,128)(2,1)} %get-tuple-element.33.refs_0_), channel_id=1, source_target_pairs={{0,4},{2,6},{4,0},{6,2},{8,12},{10,14},{12,8},{14,10},{16,20},{18,... | collective-permute-start | bytes 4718600 | tf_op jit(solution)/shard_map/L_XO/ppermute | solution.py:183
  9.4 3.8 %collective-permute-start = (bf16[384,1024]{1,0:T(8,128)(2,1)}, bf16[384,1024]{1,0:T(8,128)(2,1)}, u32[]{:S(2)}, u32[]{:S(2)}) collective-permute-start(bf16[384,1024]{1,0:T(8,128)(2,1)} %get-tuple-element.32), channel_id=1, source_target_pairs={{8,16},{10,18},{12,20},{14,22},{16,8},{18,10},{20,12},{22,14},{9,1... | collective-permute-start | bytes 2359304 | tf_op jit(solution)/shard_map/L_Qa/ppermute | solution.py:183
  11.0 10.8 %collective-permute-start.2 = (bf16[384,1024]{1,0:T(8,128)(2,1)}, bf16[384,1024]{1,0:T(8,128)(2,1)}, u32[]{:S(2)}, u32[]{:S(2)}) collective-permute-start(bf16[384,1024]{1,0:T(8,128)(2,1)} %get-tuple-element.34), channel_id=1, source_target_pairs={{8,16},{10,18},{12,20},{14,22},{16,8},{18,10},{20,12},{22,14},{9,1... | collective-permute-start | bytes 2359304 | tf_op jit(solution)/shard_map/L_Qb/ppermute | solution.py:183
  13.2 46.8 %collective-permute-start.6 = (bf16[384,1024]{1,0:T(8,128)(2,1)}, bf16[384,1024]{1,0:T(8,128)(2,1)S(1)}, u32[]{:S(2)}, u32[]{:S(2)}) collective-permute-start(bf16[384,1024]{1,0:T(8,128)(2,1)} %collective-permute-done.first_ref), channel_id=1, source_target_pairs={{8,0},{10,2},{12,4},{14,6},{16,24},{18,26},{20,28},{22,30},{9,1},{... | collective-permute-start | bytes 2359304 | tf_op jit(solution)/shard_map/L_Sa/ppermute | solution.py:183
  44.7 22.3 %collective-permute-start.10 = (bf16[768,1024]{1,0:T(8,128)(2,1)S(1)}, bf16[768,1024]{1,0:T(8,128)(2,1)S(1)}, u32[]{:S(2)}, u32[]{:S(2)}) collective-permute-start(bf16[768,1024]{1,0:T(8,128)(2,1)S(1)} %collective-permute-done.1.refs_0_), channel_id=1, source_target_pairs={{0,2},{2,0},{4,6},{6,4},{8,10},{10,8},{12,14},{14,12},{16,18},{18,... | collective-permute-start | bytes 4718600 | tf_op jit(solution)/shard_map/L_CP/ppermute | solution.py:183
  44.8 22.3 %collective-permute-start.11 = (bf16[768,1024]{1,0:T(8,128)(2,1)S(1)}, bf16[768,1024]{1,0:T(8,128)(2,1)S(1)}, u32[]{:S(2)}, u32[]{:S(2)}) collective-permute-start(bf16[768,1024]{1,0:T(8,128)(2,1)S(1)} %collective-permute-done.3.refs_1_), channel_id=1, source_target_pairs={{0,2},{2,0},{4,6},{6,4},{8,10},{10,8},{12,14},{14,12},{16,18},{18,... | collective-permute-start | bytes 4718600 | tf_op jit(solution)/shard_map/L_CXO/ppermute | solution.py:183
  45.3 19.5 %collective-permute-start.5 = (bf16[384,1024]{1,0:T(8,128)(2,1)S(1)}, bf16[384,1024]{1,0:T(8,128)(2,1)S(1)}, u32[]{:S(2)}, u32[]{:S(2)}) collective-permute-start(bf16[384,1024]{1,0:T(8,128)(2,1)S(1)} %slice.20), channel_id=1, source_target_pairs={{0,4},{2,6},{4,0},{6,2},{8,12},{10,14},{12,8},{14,10},{16,20},{18,... | collective-permute-start | bytes 2359304 | tf_op jit(solution)/shard_map/L_XPa/ppermute | solution.py:183
  46.8 37.4 %collective-permute-start.8 = (bf16[768,1024]{1,0:T(8,128)(2,1)S(1)}, bf16[768,1024]{1,0:T(8,128)(2,1)S(1)}, u32[]{:S(2)}, u32[]{:S(2)}) collective-permute-start(bf16[768,1024]{1,0:T(8,128)(2,1)S(1)} %collective-permute-done.1.refs_0_), channel_id=1, source_target_pairs={{8,16},{10,18},{12,20},{14,22},{16,8},{18,10},{20,12},{22,14},{9,1... | collective-permute-start | bytes 4718600 | tf_op jit(solution)/shard_map/L_T/ppermute | solution.py:183
  60.0 21.5 %collective-permute-start.9 = (bf16[384,1024]{1,0:T(8,128)(2,1)}, bf16[384,1024]{1,0:T(8,128)(2,1)S(1)}, u32[]{:S(2)}, u32[]{:S(2)}) collective-permute-start(bf16[384,1024]{1,0:T(8,128)(2,1)} %collective-permute-done.2.first_ref), channel_id=1, source_target_pairs={{8,0},{10,2},{12,4},{14,6},{16,24},{18,26},{20,28},{22,30},{9,1},{... | collective-permute-start | bytes 2359304 | tf_op jit(solution)/shard_map/L_Sb/ppermute | solution.py:183
  65.5 18.7 %collective-permute-start.7 = (bf16[384,1024]{1,0:T(8,128)(2,1)S(1)}, bf16[384,1024]{1,0:T(8,128)(2,1)S(1)}, u32[]{:S(2)}, u32[]{:S(2)}) collective-permute-start(bf16[384,1024]{1,0:T(8,128)(2,1)S(1)} %shard_map.49.refs_1_), channel_id=1, source_target_pairs={{0,4},{2,6},{4,0},{6,2},{8,12},{10,14},{12,8},{14,10},{16,20},{18,... | collective-permute-start | bytes 2359304 | tf_op jit(solution)/shard_map/L_XM1a/ppermute | solution.py:183
  67.0 20.8 %collective-permute-start.15 = (bf16[384,1024]{1,0:T(8,128)(2,1)S(1)}, bf16[384,1024]{1,0:T(8,128)(2,1)S(1)}, u32[]{:S(2)}, u32[]{:S(2)}) collective-permute-start(bf16[384,1024]{1,0:T(8,128)(2,1)S(1)} %shard_map.49.refs_1_), channel_id=1, source_target_pairs={{0,2},{2,0},{4,6},{6,4},{8,10},{10,8},{12,14},{14,12},{16,18},{18,... | collective-permute-start | bytes 2359304 | tf_op jit(solution)/shard_map/L_CM1a/ppermute | solution.py:183
  73.1 15.3 %collective-permute-start.14 = (bf16[384,1024]{1,0:T(8,128)(2,1)S(1)}, bf16[384,1024]{1,0:T(8,128)(2,1)S(1)}, u32[]{:S(2)}, u32[]{:S(2)}) collective-permute-start(bf16[384,1024]{1,0:T(8,128)(2,1)S(1)} %collective-permute-done.5.refs_0_), channel_id=1, source_target_pairs={{0,2},{2,0},{4,6},{6,4},{8,10},{10,8},{12,14},{14,12},{16,18},{18,... | collective-permute-start | bytes 2359304 | tf_op jit(solution)/shard_map/L_CXPa/ppermute | solution.py:183
  84.3 23.1 %collective-permute-start.13 = (bf16[384,1024]{1,0:T(8,128)(2,1)S(1)}, bf16[384,1024]{1,0:T(8,128)(2,1)S(1)}, u32[]{:S(2)}, u32[]{:S(2)}) collective-permute-start(bf16[384,1024]{1,0:T(8,128)(2,1)S(1)} %get-tuple-element.60), channel_id=1, source_target_pairs={{8,0},{10,2},{12,4},{14,6},{16,24},{18,26},{20,28},{22,30},{9,1},{... | collective-permute-start | bytes 2359304 | tf_op jit(solution)/shard_map/L_Ua/ppermute | solution.py:183
  86.3 21.1 %collective-permute-start.12 = (bf16[384,1024]{1,0:T(8,128)(2,1)S(1)}, bf16[384,1024]{1,0:T(8,128)(2,1)S(1)}, u32[]{:S(2)}, u32[]{:S(2)}) collective-permute-start(bf16[384,1024]{1,0:T(8,128)(2,1)S(1)} %shard_map.52.refs_0_), channel_id=1, source_target_pairs={{0,4},{2,6},{4,0},{6,2},{8,12},{10,14},{12,8},{14,10},{16,20},{18,... | collective-permute-start | bytes 2359304 | tf_op jit(solution)/shard_map/L_XM1b/ppermute | solution.py:183
  87.9 26.3 %collective-permute-start.19 = (bf16[384,1024]{1,0:T(8,128)(2,1)S(1)}, bf16[384,1024]{1,0:T(8,128)(2,1)S(1)}, u32[]{:S(2)}, u32[]{:S(2)}) collective-permute-start(bf16[384,1024]{1,0:T(8,128)(2,1)S(1)} %shard_map.52.refs_0_), channel_id=1, source_target_pairs={{0,2},{2,0},{4,6},{6,4},{8,10},{10,8},{12,14},{14,12},{16,18},{18,... | collective-permute-start | bytes 2359304 | tf_op jit(solution)/shard_map/L_CM1b/ppermute | solution.py:183
  87.9 22.1 %collective-permute-start.18 = (bf16[384,1024]{1,0:T(8,128)(2,1)S(1)}, bf16[384,1024]{1,0:T(8,128)(2,1)S(1)}, u32[]{:S(2)}, u32[]{:S(2)}) collective-permute-start(bf16[384,1024]{1,0:T(8,128)(2,1)S(1)} %collective-permute-done.7.refs_2_), channel_id=1, source_target_pairs={{0,2},{2,0},{4,6},{6,4},{8,10},{10,8},{12,14},{14,12},{16,18},{18,... | collective-permute-start | bytes 2359304 | tf_op jit(solution)/shard_map/L_CXM1a/ppermute | solution.py:183
  107.4 20.0 %collective-permute-start.17 = (bf16[384,1024]{1,0:T(8,128)(2,1)S(1)}, bf16[384,1024]{1,0:T(8,128)(2,1)S(1)}, u32[]{:S(2)}, u32[]{:S(2)}) collective-permute-start(bf16[384,1024]{1,0:T(8,128)(2,1)S(1)} %get-tuple-element.59), channel_id=1, source_target_pairs={{8,0},{10,2},{12,4},{14,6},{16,24},{18,26},{20,28},{22,30},{9,1},{... | collective-permute-start | bytes 2359304 | tf_op jit(solution)/shard_map/L_Ub/ppermute | solution.py:183
  109.4 18.1 %collective-permute-start.16 = (bf16[384,1024]{1,0:T(8,128)(2,1)S(1)}, bf16[384,1024]{1,0:T(8,128)(2,1)S(1)}, u32[]{:S(2)}, u32[]{:S(2)}) collective-permute-start(bf16[384,1024]{1,0:T(8,128)(2,1)S(1)} %shard_map.54.refs_0_), channel_id=1, source_target_pairs={{0,4},{2,6},{4,0},{6,2},{8,12},{10,14},{12,8},{14,10},{16,20},{18,... | collective-permute-start | bytes 2359304 | tf_op jit(solution)/shard_map/L_XM2a/ppermute | solution.py:183
  110.0 22.2 %collective-permute-start.23 = (bf16[384,1024]{1,0:T(8,128)(2,1)S(1)}, bf16[384,1024]{1,0:T(8,128)(2,1)S(1)}, u32[]{:S(2)}, u32[]{:S(2)}) collective-permute-start(bf16[384,1024]{1,0:T(8,128)(2,1)S(1)} %shard_map.54.refs_0_), channel_id=1, source_target_pairs={{0,2},{2,0},{4,6},{6,4},{8,10},{10,8},{12,14},{14,12},{16,18},{18,... | collective-permute-start | bytes 2359304 | tf_op jit(solution)/shard_map/L_CM2a/ppermute | solution.py:183
  127.4 4.7 %collective-permute-start.24 = (bf16[384,1024]{1,0:T(8,128)(2,1)S(1)}, bf16[384,1024]{1,0:T(8,128)(2,1)S(1)}, u32[]{:S(2)}, u32[]{:S(2)}) collective-permute-start(bf16[384,1024]{1,0:T(8,128)(2,1)S(1)} %collective-permute-done.16.refs_1_), channel_id=1, source_target_pairs={{0,2},{2,0},{4,6},{6,4},{8,10},{10,8},{12,14},{14,12},{16,18},{18,... | collective-permute-start | bytes 2359304 | tf_op jit(solution)/shard_map/L_CXM2a/ppermute | solution.py:183
  127.4 11.4 %collective-permute-start.22 = (bf16[384,1024]{1,0:T(8,128)(2,1)S(1)}, bf16[384,1024]{1,0:T(8,128)(2,1)S(1)}, u32[]{:S(2)}, u32[]{:S(2)}) collective-permute-start(bf16[384,1024]{1,0:T(8,128)(2,1)S(1)} %collective-permute-done.12.refs_2_), channel_id=1, source_target_pairs={{0,2},{2,0},{4,6},{6,4},{8,10},{10,8},{12,14},{14,12},{16,18},{18,... | collective-permute-start | bytes 2359304 | tf_op jit(solution)/shard_map/L_CXM1b/ppermute | solution.py:183
  128.0 20.4 %collective-permute-start.21 = (bf16[384,1024]{1,0:T(8,128)(2,1)S(1)}, bf16[384,1024]{1,0:T(8,128)(2,1)S(1)}, u32[]{:S(2)}, u32[]{:S(2)}) collective-permute-start(bf16[384,1024]{1,0:T(8,128)(2,1)S(1)} %slice.23), channel_id=1, source_target_pairs={{0,8},{2,10},{4,12},{6,14},{8,0},{10,2},{12,4},{14,6},{16,24},{18,... | collective-permute-start | bytes 2359304 | tf_op jit(solution)/shard_map/L_E/ppermute | solution.py:183
  131.6 19.2 %collective-permute-start.20 = (bf16[384,1024]{1,0:T(8,128)(2,1)S(1)}, bf16[384,1024]{1,0:T(8,128)(2,1)S(1)}, u32[]{:S(2)}, u32[]{:S(2)}) collective-permute-start(bf16[384,1024]{1,0:T(8,128)(2,1)S(1)} %shard_map.57.refs_1_), channel_id=1, source_target_pairs={{0,4},{2,6},{4,0},{6,2},{8,12},{10,14},{12,8},{14,10},{16,20},{18,... | collective-permute-start | bytes 2359304 | tf_op jit(solution)/shard_map/L_XM2b/ppermute | solution.py:183
  137.2 13.6 %collective-permute-start.25 = (bf16[2,192,512]{2,1,0:T(8,128)(2,1)S(1)}, bf16[2,192,512]{2,1,0:T(8,128)(2,1)S(1)}, u32[]{:S(2)}, u32[]{:S(2)}) collective-permute-start(bf16[2,192,512]{2,1,0:T(8,128)(2,1)S(1)} %shard_map.59), channel_id=1, source_target_pairs={{0,1},{1,0},{2,3},{3,2},{4,5},{5,4},{6,7},{7,6},{8,9},{9,8},{10,11... | collective-permute-start | bytes 1179656 | tf_op jit(solution)/shard_map/L_partial/ppermute | solution.py:254
  138.8 12.5 %collective-permute-start.28 = (bf16[384,1024]{1,0:T(8,128)(2,1)S(1)}, bf16[384,1024]{1,0:T(8,128)(2,1)S(1)}, u32[]{:S(2)}, u32[]{:S(2)}) collective-permute-start(bf16[384,1024]{1,0:T(8,128)(2,1)S(1)} %shard_map.57.refs_1_), channel_id=1, source_target_pairs={{0,2},{2,0},{4,6},{6,4},{8,10},{10,8},{12,14},{14,12},{16,18},{18,... | collective-permute-start | bytes 2359304 | tf_op jit(solution)/shard_map/L_CM2b/ppermute | solution.py:183
  150.8 5.7 %collective-permute-start.26 = (bf16[384,1024]{1,0:T(8,128)(2,1)S(1)}, bf16[384,1024]{1,0:T(8,128)(2,1)S(1)}, u32[]{:S(2)}, u32[]{:S(2)}) collective-permute-start(bf16[384,1024]{1,0:T(8,128)(2,1)S(1)} %collective-permute-done.20.refs_1_), channel_id=1, source_target_pairs={{0,2},{2,0},{4,6},{6,4},{8,10},{10,8},{12,14},{14,12},{16,18},{18,... | collective-permute-start | bytes 2359304 | tf_op jit(solution)/shard_map/L_CXM2b/ppermute | solution.py:183
  150.8 5.8 %collective-permute-start.27 = (bf16[384,1024]{1,0:T(8,128)(2,1)S(1)}, bf16[384,1024]{1,0:T(8,128)(2,1)S(1)}, u32[]{:S(2)}, u32[]{:S(2)}) collective-permute-start(bf16[384,1024]{1,0:T(8,128)(2,1)S(1)} %collective-permute-done.21.refs_2_), channel_id=1, source_target_pairs={{0,2},{2,0},{4,6},{6,4},{8,10},{10,8},{12,14},{14,12},{16,18},{18,... | collective-permute-start | bytes 2359304 | tf_op jit(solution)/shard_map/L_CE/ppermute | solution.py:183

commit v2 on v1

--- a/solution.py
+++ b/solution.py
@@ -56,7 +56,7 @@
         kernel,
         out_shape=[jax.ShapeDtypeStruct((n * columns, depth), jnp.bfloat16) for n in (2, 1, 1)],
         out_specs=[IN_VMEM] * 3,
-        compiler_params=pltpu.CompilerParams(vmem_limit_bytes=34 * 2**20),
+        compiler_params=pltpu.CompilerParams(vmem_limit_bytes=60 * 2**20),
         cost_estimate=pl.CostEstimate(flops=1000, bytes_accessed=1000, transcendentals=0),
     )(slab, beam_hkl)
 
@@ -138,6 +138,78 @@
     )(blocks, s_matrix, *pieces, *extra)
 
 
+def take(which, blocks, s_matrix, depth):
+    rows = s_matrix.shape[1]
+
+    def kernel(blocks_ref, s_ref, out_ref, done):
+        copies = []
+        for k, w in enumerate(which):
+            start = pl.multiple_of(blocks_ref[w] * depth, depth)
+            copies.append(pltpu.make_async_copy(s_ref.at[:, :, pl.ds(start, depth)], out_ref.at[k], done.at[k]))
+        for copy in copies:
+            copy.start()
+        for copy in copies:
+            copy.wait()
+
+    return pl.pallas_call(
+        kernel,
+        out_shape=jax.ShapeDtypeStruct((len(which), 2, rows, depth), s_matrix.dtype),
+        in_specs=[pl.BlockSpec(memory_space=pltpu.SMEM), pl.BlockSpec(memory_space=pltpu.HBM)],
+        out_specs=IN_VMEM,
+        scratch_shapes=[pltpu.SemaphoreType.DMA((len(which),))],
+        compiler_params=pltpu.CompilerParams(vmem_limit_bytes=34 * 2**20),
+        cost_estimate=pl.CostEstimate(flops=1000, bytes_accessed=1000, transcendentals=0),
+    )(blocks, s_matrix)
+
+
+def multiply_tiles(which, tiles, pieces, total, finish, received):
+    count = len(pieces)
+    width, depth = pieces[0].shape
+    rows = tiles.shape[2]
+    half = width // 2
+    extra = [v for v in (total, received) if v is not None]
+
+    def kernel(tiles_ref, *refs):
+        total_ref = refs[count]
+        received_ref = refs[count + 1] if received is not None else None
+        out_ref = refs[count + len(extra)]
+        sums = []
+        for part in range(2):
+            lanes = slice(part * rows, (part + 1) * rows)
+            value = total_ref[:, lanes]
+            for p in range(count):
+                value += lax.dot_general(
+                    refs[p][...], tiles_ref[which[p], part], (((1,), (1,)), ((), ())), preferred_element_type=jnp.float32
+                )
+            if finish:
+                sums.append(value)
+            else:
+                out_ref[:, lanes] = value
+        if finish:
+            real = sums[0][:half] - sums[1][half:]
+            imag = sums[0][half:] + sums[1][:half]
+            if received is not None:
+                real += received_ref[0].astype(jnp.float32)
+                imag += received_ref[1].astype(jnp.float32)
+            out_ref[0] = real.astype(out_ref.dtype)
+            out_ref[1] = imag.astype(out_ref.dtype)
+
+    out_shape = (
+        jax.ShapeDtypeStruct((2, half, rows), jnp.bfloat16)
+        if finish
+        else jax.ShapeDtypeStruct((width, 2 * rows), jnp.float32)
+    )
+    return pl.pallas_call(
+        kernel,
+        out_shape=out_shape,
+        in_specs=[IN_VMEM] * (1 + count + len(extra)),
+        out_specs=IN_VMEM,
+        input_output_aliases={} if finish else {1 + count: 0},
+        compiler_params=pltpu.CompilerParams(vmem_limit_bytes=34 * 2**20),
+        cost_estimate=pl.CostEstimate(flops=1000, bytes_accessed=1000, transcendentals=0),
+    )(tiles, *pieces, *extra)
+
+
 def choose(flag, first, second, row=0):
     rows = second.shape[0]
 
@@ -160,6 +232,31 @@
         compiler_params=pltpu.CompilerParams(vmem_limit_bytes=34 * 2**20),
         cost_estimate=pl.CostEstimate(flops=1000, bytes_accessed=1000, transcendentals=0),
     )(flag, first, second)
+
+
+def stack(*parts):
+    offsets = [sum(v.shape[0] for v in parts[:k]) for k in range(len(parts))]
+
+    def kernel(*refs):
+        out_ref, done = refs[len(parts) :]
+        copies = [
+            pltpu.make_async_copy(refs[k], out_ref.at[offsets[k] : offsets[k] + v.shape[0], :], done.at[k])
+            for k, v in enumerate(parts)
+        ]
+        for copy in copies:
+            copy.start()
+        for copy in copies:
+            copy.wait()
+
+    return pl.pallas_call(
+        kernel,
+        out_shape=jax.ShapeDtypeStruct((sum(v.shape[0] for v in parts), parts[0].shape[1]), parts[0].dtype),
+        in_specs=[pl.BlockSpec(memory_space=pl.ANY)] * len(parts),
+        out_specs=pl.BlockSpec(memory_space=pl.ANY),
+        scratch_shapes=[pltpu.SemaphoreType.DMA((len(parts),))],
+        compiler_params=pltpu.CompilerParams(vmem_limit_bytes=34 * 2**20),
+        cost_estimate=pl.CostEstimate(flops=1000, bytes_accessed=1000, transcendentals=0),
+    )(*parts)
 
 
 def line_of_four(s_matrix, slab, beam_hkl):
@@ -218,45 +315,61 @@
         return multiply([names.index(n) for n in which], here, s_matrix, pieces, total, **kw)
 
     ob = lax.optimization_barrier
-    XO, P, Qa, Qb = X(O, "O"), send(O, outer, "P"), send(Oa, middle, "Qa"), send(Ob, middle, "Qb")
+
+    def upper(v):
+        return (v, 0, v.shape[0] // 2)
+
+    def lower(v):
+        return (v, v.shape[0] // 2, v.shape[0] // 2)
+
     CO = C(O, "O")
+    XO, Pa, Qa, Pb, Qb = (
+        X(O, "O"), send(Oa, outer, "Pa"), send(Oa, middle, "Qa"), send(Ob, outer, "Pb"), send(Ob, middle, "Qb")
+    )
     AB = mul(["O", "cO"], [O, CO], None)
-    Sa = send(Qa, outward, "Sa")
-    P, Qb, XO, AB = ob((P, Qb, XO, AB))
-    XPa, Sb, T = X(P[:wide], "Pa"), send(Qb, outward, "Sb"), send(P, middle, "T")
-    CP, CXO = C(P, "P"), C(XO, "XO")
+    Pa, Qa = ob((Pa, Qa))
+    Sa, Ta = send(Qa, outward, "Sa"), send(Pa, middle, "Ta")
+    Pa, Pb, Qb, XO, AB = ob((Pa, Pb, Qb, XO, AB))
+    XPa, Sb = X(Pa, "Pa"), send(Qb, outward, "Sb")
+    CXO = C(XO, "XO")
+    P = stack(Pa, Pb)
     AB = mul(["P", "xO"], [P, XO], AB)
-    XPa, Sa, AB = ob((XPa, Sa, AB))
+    Sa, Ta, XPa, AB = ob((Sa, Ta, XPa, AB))
     M1a = choose(in_middle, Qa, Sa)
     XM1a = X(M1a, "M1a")
-    CXPa, CM1a = C(XPa, "XPa"), C(M1a, "M1a")
-    AB = mul(["cP", "xcO"], [CP, CXO], AB)
+    Tb, Ua = send(after(Pb, Sa), middle, "Tb"), send(Ta, outward, "Ua")
+    H = C(stack(XPa, M1a), "XPaM1a")
+    AB = mul(["xcO"], [CXO], AB)
     A = mul(["xP", "M"], [XPa, M1a], a(AB))
-    XM1a, T, Sb, A, AB = ob((XM1a, T, Sb, A, AB))
+    Sb, XM1a, A, AB = ob((Sb, XM1a, A, AB))
     M1b = choose(in_middle, Qb, Sb)
     XM1b = X(M1b, "M1b")
-    Ua, Ub = send(T[:wide], outward, "Ua"), send(T[wide:], outward, "Ub")
+    Ub = send(Tb, outward, "Ub")
     CXM1a, CM1b = C(XM1a, "XM1a"), C(M1b, "M1b")
-    A = mul(["xcP", "cM", "xM"], [CXPa, CM1a, XM1a], A)
-    XM1b, Ua, A = ob((XM1b, Ua, A))
-    M2a = choose(in_middle, T, Ua)
+    A = mul(["xcP", "cM", "xM"], [upper(H), lower(H), XM1a], A)
+    tiles = take([names.index(n) for n in ("xN", "xP", "xcN", "xcP")], after(here, A), s_matrix, O.shape[1])
+    Ua, XM1b, XO, A = ob((Ua, XM1b, XO, A))
+    M2a = choose(in_middle, Ta, Ua)
     XM2a = X(M2a, "M2a")
-    E = send(after(XO, Ua)[wide:], outer, "E")
+    E = send(XO[wide:], outer, "E")
     CXM1b, CM2a = C(XM1b, "XM1b"), C(M2a, "M2a")
+    CPa = C(after(Pa, M2a), "Pa")
+    A = mul(["N", "xcM"], [M2a, CXM1a], A)
     B = mul(["M", "cM", "xM"], [M1b, CM1b, XM1b], b(AB))
-    A = mul(["N", "xcM"], [M2a, CXM1a], A)
-    XM2a, Ub, A, B = ob((XM2a, Ub, A, B))
-    M2b = choose(in_middle, T, Ub, wide)
+    Ub, A, B, tiles = ob((Ub, A, B, tiles))
+    M2b = choose(in_middle, Tb, Ub)
     XM2b = X(M2b, "M2b")
+    XM2a, M2b = ob((XM2a, M2b))
     CXM2a, CM2b = C(XM2a, "XM2a"), C(M2b, "M2b")
-    partial = mul(["cN", "xN", "xcN"], [CM2a, XM2a, CXM2a], A, finish=True)
+    CPb = C(after(Pb, M2b), "Pb")
+    partial = mul(["cN", "cP", "xN", "xcN"], [CM2a, CPa, XM2a, CXM2a], A, finish=True)
     with jax.named_scope("L_partial"):
         received = lax.ppermute(partial, "col", [(0, 1), (1, 0)])
-    B = mul(["xcM", "N"], [CXM1b, M2b], B)
-    XM2b, E, B, received = ob((XM2b, E, B, received))
+    B = mul(["xcM", "cP", "N", "cN"], [CXM1b, CPb, M2b, CM2b], B)
+    XM2b, E, B, received, tiles = ob((XM2b, E, B, received, tiles))
     CXM2b, CE = C(XM2b, "XM2b"), C(E, "E")
-    B = mul(["cN", "xN", "xP"], [CM2b, XM2b, E], B)
-    out = mul(["xcN", "xcP"], [CXM2b, CE], B, finish=True, received=received)
+    B = multiply_tiles([0, 1], tiles, [XM2b, E], B, False, None)
+    out = multiply_tiles([2, 3], tiles, [CXM2b, CE], B, True, received)
     return jnp.swapaxes(out, 1, 2)
 
 

time: 162 us -> 149 us (0.920)
  waiting for transfers between devices: 68.1 us -> 33.8 us
  starting transfers between devices: 26.5 us -> 48.3 us
    ppermute x28 -> x30, waiting for transfers between devices: 68.1 us -> 33.8 us  [send(): return lax.ppermute(value, 'row', route)]
    ppermute x28 -> x30, starting transfers between devices: 24.9 us -> 46.7 us  [send(): return lax.ppermute(value, 'row', route)]
    pallas_call x11 -> x9, Pallas kernels: 57.3 us -> 46.7 us  [multiply(): pl.pallas_call(kernel, out_shape=out_shape, in_specs=[pl.BlockSpec(memory...]
    pallas_call x0 -> x5, Pallas kernels: none -> 10.1 us  [the longest x2 4.52 us: multiply_tiles(): pl.pallas_call(kernel, out_shape=out_shape, in_specs=[IN_VMEM] * (1 + cou...]
  transfers between devices with their start and end apart: 29 -> 31, of which waited for: 10 -> 11; matrix products, arithmetic and copies ran while one was open for 1% -> 1% of each run, Pallas kernels for 34% -> 38%
where the time goes in v2:
time: 149 us
  Pallas kernels  63.8 us (43%)
  starting transfers between devices  48.3 us (32%)
  waiting for transfers between devices  33.8 us (23%)
  local copies, waits for them, and re-layouts  2.72 us (2%)
    ppermute x30, starting transfers between devices, send(): return lax.ppermute(value, 'row', route)  46.7 us
    pallas_call x9, Pallas kernels, multiply(): pl.pallas_call(kernel, out_shape=out_shape, in_specs=[pl.BlockSpec(memory...  46.7 us
    ppermute x30, waiting for transfers between devices, send(): return lax.ppermute(value, 'row', route)  33.8 us
    pallas_call x2, Pallas kernels, multiply_tiles(): pl.pallas_call(kernel, out_shape=out_shape, in_specs=[IN_VMEM] * (1 + cou...  4.52 us
    pallas_call x1, Pallas kernels, phase_panels(): pl.pallas_call(kernel, out_shape=[jax.ShapeDtypeStruct((n * columns, dept...  4.16 us
    pallas_call x1, Pallas kernels, take(): pl.pallas_call(kernel, out_shape=jax.ShapeDtypeStruct((len(which), 2, row...  4.07 us
  transfers between devices with their start and end apart: 31, of which 11 were waited for; matrix products, arithmetic and copies ran while one was open for 1% of the time, Pallas kernels for 38%

profile of v2, /device:TPU:0, one launch (start us, length us, event | category | flops | bytes accessed | tf_op | source)
XLA Modules:
  0.0 148.9 jit_solution(6856453344136334125)
XLA Ops:
  0.0 4.2 %shard_map.46 = (bf16[768,1024]{1,0:T(8,128)(2,1)}, bf16[384,1024]{1,0:T(8,128)(2,1)}, bf16[384,1024]{1,0:T(8,128)(2,1)}) custom-call(bf16[2,1024,384]{2,1,0:T(8,128)(2,1)} %slab_ref.1, s32[3,1024]{1,0:T(4,128)} %hkl_ref.1), custom_call_target="tpu_custom_call" | custom-call | flops 1000 | bytes 1000 | tf_op jit(solution)/shard_map/pallas_call | solution.py:55
  4.6 1.6 %collective-permute-start.1 = (bf16[384,1024]{1,0:T(8,128)(2,1)}, bf16[384,1024]{1,0:T(8,128)(2,1)}, u32[]{:S(2)}, u32[]{:S(2)}) collective-permute-start(bf16[384,1024]{1,0:T(8,128)(2,1)} %get-tuple-element.42), channel_id=1, source_target_pairs={{8,16},{10,18},{12,20},{14,22},{16,8},{18,10},{20,12},{22,14},{9,1... | collective-permute-start | bytes 2359304 | tf_op jit(solution)/shard_map/L_Qa/ppermute | solution.py:280
  6.2 2.5 %collective-permute-start.4 = (bf16[768,1024]{1,0:T(8,128)(2,1)}, bf16[768,1024]{1,0:T(8,128)(2,1)S(1)}, u32[]{:S(2)}, u32[]{:S(2)}) collective-permute-start(bf16[768,1024]{1,0:T(8,128)(2,1)} %get-tuple-element.45.refs_0_), channel_id=1, source_target_pairs={{0,4},{2,6},{4,0},{6,2},{8,12},{10,14},{12,8},{14,10},{16,20},{18,... | collective-permute-start | bytes 4718600 | tf_op jit(solution)/shard_map/L_XO/ppermute | solution.py:280
  8.7 3.5 %collective-permute-start = (bf16[384,1024]{1,0:T(8,128)(2,1)}, bf16[384,1024]{1,0:T(8,128)(2,1)}, u32[]{:S(2)}, u32[]{:S(2)}) collective-permute-start(bf16[384,1024]{1,0:T(8,128)(2,1)} %get-tuple-element.42), channel_id=1, source_target_pairs={{0,8},{2,10},{4,12},{6,14},{8,0},{10,2},{12,4},{14,6},{16,24},{18,... | collective-permute-start | bytes 2359304 | tf_op jit(solution)/shard_map/L_Pa/ppermute | solution.py:280
  12.2 1.6 %collective-permute-start.3 = (bf16[384,1024]{1,0:T(8,128)(2,1)}, bf16[384,1024]{1,0:T(8,128)(2,1)}, u32[]{:S(2)}, u32[]{:S(2)}) collective-permute-start(bf16[384,1024]{1,0:T(8,128)(2,1)} %get-tuple-element.44), channel_id=1, source_target_pairs={{8,16},{10,18},{12,20},{14,22},{16,8},{18,10},{20,12},{22,14},{9,1... | collective-permute-start | bytes 2359304 | tf_op jit(solution)/shard_map/L_Qb/ppermute | solution.py:280
  13.8 15.9 %collective-permute-start.2 = (bf16[384,1024]{1,0:T(8,128)(2,1)}, bf16[384,1024]{1,0:T(8,128)(2,1)}, u32[]{:S(2)}, u32[]{:S(2)}) collective-permute-start(bf16[384,1024]{1,0:T(8,128)(2,1)} %get-tuple-element.44), channel_id=1, source_target_pairs={{0,8},{2,10},{4,12},{6,14},{8,0},{10,2},{12,4},{14,6},{16,24},{18,... | collective-permute-start | bytes 2359304 | tf_op jit(solution)/shard_map/L_Pb/ppermute | solution.py:280
  29.7 0.7 fusion
  30.4 0.7 collective-permute-start.7
  31.1 1.3 collective-permute-start.6
  32.5 1.4 copy-done
  33.9 5.9 %shard_map.47.refs_2_ = f32[768,1024]{1,0:T(8,128)S(1)} custom-call(s32[17]{0:T(128)S(1)} %get-tuple-element.64.blocks_ref, bf16[2,512,16384]{2,1,0:T(8,128)(2,1)} %s_ref.19, bf16[768,1024]{1,0:T(8,128)(2,1)S(1)} %copy-done, bf16[768,1024]{1,0:T(8,128)(2,1)S(1)} %collective-permute-done.5.refs_1_), custom_call_target="tpu_custom_call" | custom-call | flops 1000 | bytes 1000 | tf_op jit(solution)/shard_map/pallas_call | solution.py:128
  39.8 8.7 %collective-permute-done.2.refs_1_ = bf16[384,1024]{1,0:T(8,128)(2,1)} collective-permute-done((bf16[384,1024]{1,0:T(8,128)(2,1)}, bf16[384,1024]{1,0:T(8,128)(2,1)}, u32[]{:S(2)}, u32[]{:S(2)}) %collective-permute-start.2) | collective-permute-done | bytes 786464 | tf_op jit(solution)/shard_map/L_Pb/ppermute | solution.py:280
  48.5 1.5 %collective-permute-start.8 = (bf16[384,1024]{1,0:T(8,128)(2,1)}, bf16[384,1024]{1,0:T(8,128)(2,1)S(1)}, u32[]{:S(2)}, u32[]{:S(2)}) collective-permute-start(bf16[384,1024]{1,0:T(8,128)(2,1)} %collective-permute-done.refs_0_), channel_id=1, source_target_pairs={{0,4},{2,6},{4,0},{6,2},{8,12},{10,14},{12,8},{14,10},{16,20},{18,... | collective-permute-start | bytes 2359304 | tf_op jit(solution)/shard_map/L_XPa/ppermute | solution.py:280
  50.0 0.6 slice.9
  50.6 1.3 collective-permute-start.12
  51.8 1.4 shard_map.48.refs_0_
  53.2 6.0 %shard_map.49.refs_1_ = f32[768,1024]{1,0:T(8,128)S(1)} custom-call(s32[17]{0:T(128)S(1)} %get-tuple-element.64.blocks_ref, bf16[2,512,16384]{2,1,0:T(8,128)(2,1)} %s_ref.19, bf16[768,1024]{1,0:T(8,128)(2,1)S(1)} %shard_map.48.refs_0_, bf16[768,1024]{1,0:T(8,128)(2,1)S(1)} %collective-permute-done.4.refs_1_, ...), custom_call_target="tpu_custom_call", output_to_operand_aliasing={{}: (4, {})} | custom-call | flops 1000 | bytes 1000 | tf_op jit(solution)/shard_map/pallas_call | solution.py:128
  59.3 6.0 %collective-permute-done.6.second_ref = bf16[384,1024]{1,0:T(8,128)(2,1)S(1)} collective-permute-done((bf16[384,1024]{1,0:T(8,128)(2,1)}, bf16[384,1024]{1,0:T(8,128)(2,1)S(1)}, u32[]{:S(2)}, u32[]{:S(2)}) %collective-permute-start.6) | collective-permute-done | bytes 786464 | tf_op jit(solution)/shard_map/L_Sa/ppermute | solution.py:280
  65.5 0.7 shard_map.50.refs_1_
  66.1 1.6 %collective-permute-start.13 = (bf16[384,1024]{1,0:T(8,128)(2,1)S(1)}, bf16[384,1024]{1,0:T(8,128)(2,1)S(1)}, u32[]{:S(2)}, u32[]{:S(2)}) collective-permute-start(bf16[384,1024]{1,0:T(8,128)(2,1)S(1)} %shard_map.50.refs_1_), channel_id=1, source_target_pairs={{0,4},{2,6},{4,0},{6,2},{8,12},{10,14},{12,8},{14,10},{16,20},{18,... | collective-permute-start | bytes 2359304 | tf_op jit(solution)/shard_map/L_XM1a/ppermute | solution.py:280
  67.9 0.7 collective-permute-start.9
  68.6 3.9 %shard_map.51.refs_2_.refs_3_ = f32[768,1024]{1,0:T(8,128)S(1)} custom-call(s32[17]{0:T(128)S(1)} %get-tuple-element.64.blocks_ref, bf16[2,512,16384]{2,1,0:T(8,128)(2,1)} %s_ref.19, bf16[768,1024]{1,0:T(8,128)(2,1)S(1)} %collective-permute-done.14.refs_0_, f32[768,1024]{1,0:T(8,128)S(1)} %shard_map.49.refs_1_), custom_call_target="tpu_custom_call", output_to_operand_aliasing={{}: (3, {})} | custom-call | flops 1000 | bytes 1000 | tf_op jit(solution)/shard_map/pallas_call | solution.py:128
  72.6 1.5 collective-permute-start.11
  74.0 4.1 %shard_map.52.refs_3_ = f32[384,1024]{1,0:T(8,128)S(1)} custom-call(s32[17]{0:T(128)S(1)} %get-tuple-element.64.blocks_ref, bf16[2,512,16384]{2,1,0:T(8,128)(2,1)} %s_ref.19, bf16[384,1024]{1,0:T(8,128)(2,1)S(1)} %collective-permute-done.8.refs_0_, bf16[384,1024]{1,0:T(8,128)(2,1)S(1)} %shard_map.50.refs_1_, f32[768,1024]{1,0:T(8,128)S(1)} %shard_map.51.refs_2_.refs_3_), custom_call_target="tpu_custom_call" | custom-call | flops 1000 | bytes 1000 | tf_op jit(solution)/shard_map/pallas_call | solution.py:128
  78.2 2.9 %collective-permute-done.12.second_ref = bf16[384,1024]{1,0:T(8,128)(2,1)S(1)} collective-permute-done((bf16[384,1024]{1,0:T(8,128)(2,1)}, bf16[384,1024]{1,0:T(8,128)(2,1)S(1)}, u32[]{:S(2)}, u32[]{:S(2)}) %collective-permute-start.12) | collective-permute-done | bytes 786464 | tf_op jit(solution)/shard_map/L_Sb/ppermute | solution.py:280
  81.1 1.7 %collective-permute-done.13.refs_2_ = bf16[384,1024]{1,0:T(8,128)(2,1)S(1)} collective-permute-done((bf16[384,1024]{1,0:T(8,128)(2,1)S(1)}, bf16[384,1024]{1,0:T(8,128)(2,1)S(1)}, u32[]{:S(2)}, u32[]{:S(2)}) %collective-permute-start.13) | collective-permute-done | bytes 786464 | tf_op jit(solution)/shard_map/L_XM1a/ppermute | solution.py:280
  82.7 0.7 shard_map.53.refs_0_
  83.4 1.6 %collective-permute-start.15 = (bf16[384,1024]{1,0:T(8,128)(2,1)S(1)}, bf16[384,1024]{1,0:T(8,128)(2,1)S(1)}, u32[]{:S(2)}, u32[]{:S(2)}) collective-permute-start(bf16[384,1024]{1,0:T(8,128)(2,1)S(1)} %shard_map.53.refs_0_), channel_id=1, source_target_pairs={{0,4},{2,6},{4,0},{6,2},{8,12},{10,14},{12,8},{14,10},{16,20},{18,... | collective-permute-start | bytes 2359304 | tf_op jit(solution)/shard_map/L_XM1b/ppermute | solution.py:280
  85.5 1.3 collective-permute-start.10
  86.8 5.2 %shard_map.55.refs_2_ = f32[384,1024]{1,0:T(8,128)S(1)} custom-call(s32[17]{0:T(128)S(1)} %get-tuple-element.64.blocks_ref, bf16[2,512,16384]{2,1,0:T(8,128)(2,1)} %s_ref.19, bf16[768,1024]{1,0:T(8,128)(2,1)S(1)} %collective-permute-done.16.refs_0_.refs_1_, ...), custom_call_target="tpu_custom_call", output_to_operand_aliasing={{}: (5, {})} | custom-call | flops 1000 | bytes 1000 | tf_op jit(solution)/shard_map/pallas_call | solution.py:128
  92.0 5.9 %collective-permute-done.11.second_ref = bf16[384,1024]{1,0:T(8,128)(2,1)S(1)} collective-permute-done((bf16[384,1024]{1,0:T(8,128)(2,1)S(1)}, bf16[384,1024]{1,0:T(8,128)(2,1)S(1)}, u32[]{:S(2)}, u32[]{:S(2)}) %collective-permute-start.11) | collective-permute-done | bytes 786464 | tf_op jit(solution)/shard_map/L_Ua/ppermute | solution.py:280
  97.9 1.7 %collective-permute-done.15.refs_2_ = bf16[384,1024]{1,0:T(8,128)(2,1)S(1)} collective-permute-done((bf16[384,1024]{1,0:T(8,128)(2,1)S(1)}, bf16[384,1024]{1,0:T(8,128)(2,1)S(1)}, u32[]{:S(2)}, u32[]{:S(2)}) %collective-permute-start.15) | collective-permute-done | bytes 786464 | tf_op jit(solution)/shard_map/L_XM1b/ppermute | solution.py:280
  99.6 0.7 shard_map.56.refs_0_
  100.3 1.6 %collective-permute-start.22 = (bf16[384,1024]{1,0:T(8,128)(2,1)S(1)}, bf16[384,1024]{1,0:T(8,128)(2,1)S(1)}, u32[]{:S(2)}, u32[]{:S(2)}) collective-permute-start(bf16[384,1024]{1,0:T(8,128)(2,1)S(1)} %shard_map.56.refs_0_), channel_id=1, source_target_pairs={{0,4},{2,6},{4,0},{6,2},{8,12},{10,14},{12,8},{14,10},{16,20},{18,... | collective-permute-start | bytes 2359304 | tf_op jit(solution)/shard_map/L_XM2a/ppermute | solution.py:280
  101.8 4.1 %shard_map.59.tiles_ref = bf16[4,2,512,1024]{3,2,1,0:T(8,128)(2,1)S(1)} custom-call(s32[17]{0:T(128)S(1)} %get-tuple-element.64.blocks_ref, bf16[2,512,16384]{2,1,0:T(8,128)(2,1)} %s_ref.19), custom_call_target="tpu_custom_call" | custom-call | flops 1000 | bytes 1000 | tf_op jit(solution)/shard_map/pallas_call | solution.py:154
  106.5 4.2 %shard_map.57.refs_4_ = f32[384,1024]{1,0:T(8,128)S(1)} custom-call(s32[17]{0:T(128)S(1)} %get-tuple-element.64.blocks_ref, bf16[2,512,16384]{2,1,0:T(8,128)(2,1)} %s_ref.19, bf16[384,1024]{1,0:T(8,128)(2,1)S(1)} %shard_map.56.refs_0_, bf16[384,1024]{1,0:T(8,128)(2,1)S(1)} %collective-permute-done.17.refs_1_, ...), custom_call_target="tpu_custom_call", output_to_operand_aliasing={{}: (4, {})} | custom-call | flops 1000 | bytes 1000 | tf_op jit(solution)/shard_map/pallas_call | solution.py:128
  110.7 5.1 %shard_map.58.refs_4_ = f32[384,1024]{1,0:T(8,128)S(1)} custom-call(s32[17]{0:T(128)S(1)} %get-tuple-element.64.blocks_ref, bf16[2,512,16384]{2,1,0:T(8,128)(2,1)} %s_ref.19, bf16[384,1024]{1,0:T(8,128)(2,1)S(1)} %shard_map.53.refs_0_, bf16[384,1024]{1,0:T(8,128)(2,1)S(1)} %collective-permute-done.18.refs_1_, ...), custom_call_target="tpu_custom_call" | custom-call | flops 1000 | bytes 1000 | tf_op jit(solution)/shard_map/pallas_call | solution.py:128
  115.8 0.9 shard_map.60.refs_2_
  116.7 0.7 collective-permute-done.22.refs_2_
  118.6 5.0 %collective-permute-start.20 = (bf16[384,1024]{1,0:T(8,128)(2,1)S(1)}, bf16[384,1024]{1,0:T(8,128)(2,1)S(1)}, u32[]{:S(2)}, u32[]{:S(2)}) collective-permute-start(bf16[384,1024]{1,0:T(8,128)(2,1)S(1)} %slice.11), channel_id=1, source_target_pairs={{0,8},{2,10},{4,12},{6,14},{8,0},{10,2},{12,4},{14,6},{16,24},{18,... | collective-permute-start | bytes 2359304 | tf_op jit(solution)/shard_map/L_E/ppermute | solution.py:280
  124.1 6.0 %shard_map.62 = bf16[2,192,512]{2,1,0:T(8,128)(2,1)S(1)} custom-call(s32[17]{0:T(128)S(1)} %get-tuple-element.64.blocks_ref, bf16[2,512,16384]{2,1,0:T(8,128)(2,1)} %s_ref.19, bf16[384,1024]{1,0:T(8,128)(2,1)S(1)} %collective-permute-done.25.refs_0_, bf16[384,1024]{1,0:T(8,128)(2,1)S(1)} %collective-permute-done.26.refs_1_, ...), custom_call_target="tpu_custom_call" | custom-call | flops 1000 | bytes 1000 | tf_op jit(solution)/shard_map/pallas_call | solution.py:128
  130.2 1.6 %collective-permute-start.28 = (bf16[2,192,512]{2,1,0:T(8,128)(2,1)S(1)}, bf16[2,192,512]{2,1,0:T(8,128)(2,1)S(1)}, u32[]{:S(2)}, u32[]{:S(2)}) collective-permute-start(bf16[2,192,512]{2,1,0:T(8,128)(2,1)S(1)} %shard_map.62), channel_id=1, source_target_pairs={{0,1},{1,0},{2,3},{3,2},{4,5},{5,4},{6,7},{7,6},{8,9},{9,8},{10,11... | collective-permute-start | bytes 1179656 | tf_op jit(solution)/shard_map/L_partial/ppermute | solution.py:367
  131.7 6.2 %shard_map.61.refs_2_ = f32[384,1024]{1,0:T(8,128)S(1)} custom-call(s32[17]{0:T(128)S(1)} %get-tuple-element.64.blocks_ref, bf16[2,512,16384]{2,1,0:T(8,128)(2,1)} %s_ref.19, bf16[384,1024]{1,0:T(8,128)(2,1)S(1)} %collective-permute-done.21.refs_0_, bf16[384,1024]{1,0:T(8,128)(2,1)S(1)} %collective-permute-done.23.refs_1_, ...), custom_call_target="tpu_custom_call", output_to_operand_aliasing={{}: (6, {})} | custom-call | flops 1000 | bytes 1000 | tf_op jit(solution)/shard_map/pallas_call | solution.py:128
  137.9 3.5 %collective-permute-done.20.refs_1_ = bf16[384,1024]{1,0:T(8,128)(2,1)S(1)} collective-permute-done((bf16[384,1024]{1,0:T(8,128)(2,1)S(1)}, bf16[384,1024]{1,0:T(8,128)(2,1)S(1)}, u32[]{:S(2)}, u32[]{:S(2)}) %collective-permute-start.20) | collective-permute-done | bytes 786464 | tf_op jit(solution)/shard_map/L_E/ppermute | solution.py:280
  141.4 1.5 collective-permute-done.19.refs_0_
  143.4 1.9 %shard_map.63.refs_2_ = f32[384,1024]{1,0:T(8,128)S(1)} custom-call(bf16[4,2,512,1024]{3,2,1,0:T(8,128)(2,1)S(1)} %shard_map.59.tiles_ref, bf16[384,1024]{1,0:T(8,128)(2,1)S(1)} %collective-permute-done.19.refs_0_, bf16[384,1024]{1,0:T(8,128)(2,1)S(1)} %collective-permute-done.20.refs_1_, ...), custom_call_target="tpu_custom_call", output_to_operand_aliasing={{}: (3, {})} | custom-call | flops 1000 | bytes 1000 | tf_op jit(solution)/shard_map/pallas_call | solution.py:202
  145.3 1.0 collective-permute-done.30.refs_1_
  146.3 2.6 %shard_map.64 = bf16[2,192,512]{2,1,0:T(8,128)(2,1)} custom-call(bf16[4,2,512,1024]{3,2,1,0:T(8,128)(2,1)S(1)} %shard_map.59.tiles_ref, bf16[384,1024]{1,0:T(8,128)(2,1)S(1)} %collective-permute-done.29.refs_0_, bf16[384,1024]{1,0:T(8,128)(2,1)S(1)} %collective-permute-done.30.refs_1_, f32[384,1024]{1,0:T(8,128)S(1)} %shard_map.63.refs_2_, ...), custom_call_target="tpu_custom_call" | custom-call | flops 1000 | bytes 1000 | tf_op jit(solution)/shard_map/pallas_call | solution.py:202
  (38 shorter events, 4.2 us)
Async XLA Ops:
  4.2 27.0 %collective-permute-start.5 = (bf16[768,1024]{1,0:T(8,128)(2,1)}, bf16[768,1024]{1,0:T(8,128)(2,1)S(1)}, u32[]{:S(2)}, u32[]{:S(2)}) collective-permute-start(bf16[768,1024]{1,0:T(8,128)(2,1)} %get-tuple-element.45.refs_0_), channel_id=1, source_target_pairs={{0,2},{2,0},{4,6},{6,4},{8,10},{10,8},{12,14},{14,12},{16,18},{18,... | collective-permute-start | bytes 4718600 | tf_op jit(solution)/shard_map/L_CO/ppermute | solution.py:280
  4.6 9.2 %collective-permute-start.1 = (bf16[384,1024]{1,0:T(8,128)(2,1)}, bf16[384,1024]{1,0:T(8,128)(2,1)}, u32[]{:S(2)}, u32[]{:S(2)}) collective-permute-start(bf16[384,1024]{1,0:T(8,128)(2,1)} %get-tuple-element.42), channel_id=1, source_target_pairs={{8,16},{10,18},{12,20},{14,22},{16,8},{18,10},{20,12},{22,14},{9,1... | collective-permute-start | bytes 2359304 | tf_op jit(solution)/shard_map/L_Qa/ppermute | solution.py:280
  6.2 42.3 %collective-permute-start.4 = (bf16[768,1024]{1,0:T(8,128)(2,1)}, bf16[768,1024]{1,0:T(8,128)(2,1)S(1)}, u32[]{:S(2)}, u32[]{:S(2)}) collective-permute-start(bf16[768,1024]{1,0:T(8,128)(2,1)} %get-tuple-element.45.refs_0_), channel_id=1, source_target_pairs={{0,4},{2,6},{4,0},{6,2},{8,12},{10,14},{12,8},{14,10},{16,20},{18,... | collective-permute-start | bytes 4718600 | tf_op jit(solution)/shard_map/L_XO/ppermute | solution.py:280
  8.7 21.7 %collective-permute-start = (bf16[384,1024]{1,0:T(8,128)(2,1)}, bf16[384,1024]{1,0:T(8,128)(2,1)}, u32[]{:S(2)}, u32[]{:S(2)}) collective-permute-start(bf16[384,1024]{1,0:T(8,128)(2,1)} %get-tuple-element.42), channel_id=1, source_target_pairs={{0,8},{2,10},{4,12},{6,14},{8,0},{10,2},{12,4},{14,6},{16,24},{18,... | collective-permute-start | bytes 2359304 | tf_op jit(solution)/shard_map/L_Pa/ppermute | solution.py:280
  12.2 27.5 %collective-permute-start.3 = (bf16[384,1024]{1,0:T(8,128)(2,1)}, bf16[384,1024]{1,0:T(8,128)(2,1)}, u32[]{:S(2)}, u32[]{:S(2)}) collective-permute-start(bf16[384,1024]{1,0:T(8,128)(2,1)} %get-tuple-element.44), channel_id=1, source_target_pairs={{8,16},{10,18},{12,20},{14,22},{16,8},{18,10},{20,12},{22,14},{9,1... | collective-permute-start | bytes 2359304 | tf_op jit(solution)/shard_map/L_Qb/ppermute | solution.py:280
  13.8 34.7 %collective-permute-start.2 = (bf16[384,1024]{1,0:T(8,128)(2,1)}, bf16[384,1024]{1,0:T(8,128)(2,1)}, u32[]{:S(2)}, u32[]{:S(2)}) collective-permute-start(bf16[384,1024]{1,0:T(8,128)(2,1)} %get-tuple-element.44), channel_id=1, source_target_pairs={{0,8},{2,10},{4,12},{6,14},{8,0},{10,2},{12,4},{14,6},{16,24},{18,... | collective-permute-start | bytes 2359304 | tf_op jit(solution)/shard_map/L_Pb/ppermute | solution.py:280
  30.4 28.8 %collective-permute-start.7 = (bf16[384,1024]{1,0:T(8,128)(2,1)}, bf16[384,1024]{1,0:T(8,128)(2,1)S(1)}, u32[]{:S(2)}, u32[]{:S(2)}) collective-permute-start(bf16[384,1024]{1,0:T(8,128)(2,1)} %collective-permute-done.refs_0_), channel_id=1, source_target_pairs={{8,16},{10,18},{12,20},{14,22},{16,8},{18,10},{20,12},{22,14},{9,1... | collective-permute-start | bytes 2359304 | tf_op jit(solution)/shard_map/L_Ta/ppermute | solution.py:280
  31.1 34.1 %collective-permute-start.6 = (bf16[384,1024]{1,0:T(8,128)(2,1)}, bf16[384,1024]{1,0:T(8,128)(2,1)S(1)}, u32[]{:S(2)}, u32[]{:S(2)}) collective-permute-start(bf16[384,1024]{1,0:T(8,128)(2,1)} %collective-permute-done.1.first_ref), channel_id=1, source_target_pairs={{8,0},{10,2},{12,4},{14,6},{16,24},{18,26},{20,28},{22,30},{9,1},{... | collective-permute-start | bytes 2359304 | tf_op jit(solution)/shard_map/L_Sa/ppermute | solution.py:280
  32.4 1.4 copy-start
  48.5 17.0 %collective-permute-start.8 = (bf16[384,1024]{1,0:T(8,128)(2,1)}, bf16[384,1024]{1,0:T(8,128)(2,1)S(1)}, u32[]{:S(2)}, u32[]{:S(2)}) collective-permute-start(bf16[384,1024]{1,0:T(8,128)(2,1)} %collective-permute-done.refs_0_), channel_id=1, source_target_pairs={{0,4},{2,6},{4,0},{6,2},{8,12},{10,14},{12,8},{14,10},{16,20},{18,... | collective-permute-start | bytes 2359304 | tf_op jit(solution)/shard_map/L_XPa/ppermute | solution.py:280
  50.0 18.7 %collective-permute-start.14 = (bf16[768,1024]{1,0:T(8,128)(2,1)S(1)}, bf16[768,1024]{1,0:T(8,128)(2,1)S(1)}, u32[]{:S(2)}, u32[]{:S(2)}) collective-permute-start(bf16[768,1024]{1,0:T(8,128)(2,1)S(1)} %collective-permute-done.4.refs_1_), channel_id=1, source_target_pairs={{0,2},{2,0},{4,6},{6,4},{8,10},{10,8},{12,14},{14,12},{16,18},{18,... | collective-permute-start | bytes 4718600 | tf_op jit(solution)/shard_map/L_CXO/ppermute | solution.py:280
  50.6 30.5 %collective-permute-start.12 = (bf16[384,1024]{1,0:T(8,128)(2,1)}, bf16[384,1024]{1,0:T(8,128)(2,1)S(1)}, u32[]{:S(2)}, u32[]{:S(2)}) collective-permute-start(bf16[384,1024]{1,0:T(8,128)(2,1)} %collective-permute-done.3.first_ref), channel_id=1, source_target_pairs={{8,0},{10,2},{12,4},{14,6},{16,24},{18,26},{20,28},{22,30},{9,1},{... | collective-permute-start | bytes 2359304 | tf_op jit(solution)/shard_map/L_Sb/ppermute | solution.py:280
  66.1 16.6 %collective-permute-start.13 = (bf16[384,1024]{1,0:T(8,128)(2,1)S(1)}, bf16[384,1024]{1,0:T(8,128)(2,1)S(1)}, u32[]{:S(2)}, u32[]{:S(2)}) collective-permute-start(bf16[384,1024]{1,0:T(8,128)(2,1)S(1)} %shard_map.50.refs_1_), channel_id=1, source_target_pairs={{0,4},{2,6},{4,0},{6,2},{8,12},{10,14},{12,8},{14,10},{16,20},{18,... | collective-permute-start | bytes 2359304 | tf_op jit(solution)/shard_map/L_XM1a/ppermute | solution.py:280
  67.8 17.7 %collective-permute-start.16 = (bf16[768,1024]{1,0:T(8,128)(2,1)S(1)}, bf16[768,1024]{1,0:T(8,128)(2,1)S(1)}, u32[]{:S(2)}, u32[]{:S(2)}) collective-permute-start(bf16[768,1024]{1,0:T(8,128)(2,1)S(1)} %shard_map.54), channel_id=1, source_target_pairs={{0,2},{2,0},{4,6},{6,4},{8,10},{10,8},{12,14},{14,12},{16,18},{18,... | collective-permute-start | bytes 4718600 | tf_op jit(solution)/shard_map/L_CXPaM1a/ppermute | solution.py:280
  67.9 17.1 %collective-permute-start.9 = (bf16[384,1024]{1,0:T(8,128)(2,1)}, bf16[384,1024]{1,0:T(8,128)(2,1)S(1)}, u32[]{:S(2)}, u32[]{:S(2)}) collective-permute-start(bf16[384,1024]{1,0:T(8,128)(2,1)} %collective-permute-done.2.refs_1_), channel_id=1, source_target_pairs={{8,16},{10,18},{12,20},{14,22},{16,8},{18,10},{20,12},{22,14},{9,1... | collective-permute-start | bytes 2359304 | tf_op jit(solution)/shard_map/L_Tb/ppermute | solution.py:280
  72.6 25.4 %collective-permute-start.11 = (bf16[384,1024]{1,0:T(8,128)(2,1)S(1)}, bf16[384,1024]{1,0:T(8,128)(2,1)S(1)}, u32[]{:S(2)}, u32[]{:S(2)}) collective-permute-start(bf16[384,1024]{1,0:T(8,128)(2,1)S(1)} %collective-permute-done.7.first_ref), channel_id=1, source_target_pairs={{8,0},{10,2},{12,4},{14,6},{16,24},{18,26},{20,28},{22,30},{9,1},{... | collective-permute-start | bytes 2359304 | tf_op jit(solution)/shard_map/L_Ua/ppermute | solution.py:280
  83.4 16.2 %collective-permute-start.15 = (bf16[384,1024]{1,0:T(8,128)(2,1)S(1)}, bf16[384,1024]{1,0:T(8,128)(2,1)S(1)}, u32[]{:S(2)}, u32[]{:S(2)}) collective-permute-start(bf16[384,1024]{1,0:T(8,128)(2,1)S(1)} %shard_map.53.refs_0_), channel_id=1, source_target_pairs={{0,4},{2,6},{4,0},{6,2},{8,12},{10,14},{12,8},{14,10},{16,20},{18,... | collective-permute-start | bytes 2359304 | tf_op jit(solution)/shard_map/L_XM1b/ppermute | solution.py:280
  85.0 20.9 %collective-permute-start.17 = (bf16[384,1024]{1,0:T(8,128)(2,1)S(1)}, bf16[384,1024]{1,0:T(8,128)(2,1)S(1)}, u32[]{:S(2)}, u32[]{:S(2)}) collective-permute-start(bf16[384,1024]{1,0:T(8,128)(2,1)S(1)} %collective-permute-done.13.refs_2_), channel_id=1, source_target_pairs={{0,2},{2,0},{4,6},{6,4},{8,10},{10,8},{12,14},{14,12},{16,18},{18,... | collective-permute-start | bytes 2359304 | tf_op jit(solution)/shard_map/L_CXM1a/ppermute | solution.py:280
  85.0 25.7 %collective-permute-start.18 = (bf16[384,1024]{1,0:T(8,128)(2,1)S(1)}, bf16[384,1024]{1,0:T(8,128)(2,1)S(1)}, u32[]{:S(2)}, u32[]{:S(2)}) collective-permute-start(bf16[384,1024]{1,0:T(8,128)(2,1)S(1)} %shard_map.53.refs_0_), channel_id=1, source_target_pairs={{0,2},{2,0},{4,6},{6,4},{8,10},{10,8},{12,14},{14,12},{16,18},{18,... | collective-permute-start | bytes 2359304 | tf_op jit(solution)/shard_map/L_CM1b/ppermute | solution.py:280
  85.5 30.4 %collective-permute-start.10 = (bf16[384,1024]{1,0:T(8,128)(2,1)S(1)}, bf16[384,1024]{1,0:T(8,128)(2,1)S(1)}, u32[]{:S(2)}, u32[]{:S(2)}) collective-permute-start(bf16[384,1024]{1,0:T(8,128)(2,1)S(1)} %collective-permute-done.9.first_ref), channel_id=1, source_target_pairs={{8,0},{10,2},{12,4},{14,6},{16,24},{18,26},{20,28},{22,30},{9,1},{... | collective-permute-start | bytes 2359304 | tf_op jit(solution)/shard_map/L_Ub/ppermute | solution.py:280
  100.3 17.2 %collective-permute-start.22 = (bf16[384,1024]{1,0:T(8,128)(2,1)S(1)}, bf16[384,1024]{1,0:T(8,128)(2,1)S(1)}, u32[]{:S(2)}, u32[]{:S(2)}) collective-permute-start(bf16[384,1024]{1,0:T(8,128)(2,1)S(1)} %shard_map.56.refs_0_), channel_id=1, source_target_pairs={{0,4},{2,6},{4,0},{6,2},{8,12},{10,14},{12,8},{14,10},{16,20},{18,... | collective-permute-start | bytes 2359304 | tf_op jit(solution)/shard_map/L_XM2a/ppermute | solution.py:280
  101.8 16.8 %collective-permute-start.25 = (bf16[384,1024]{1,0:T(8,128)(2,1)S(1)}, bf16[384,1024]{1,0:T(8,128)(2,1)S(1)}, u32[]{:S(2)}, u32[]{:S(2)}) collective-permute-start(bf16[384,1024]{1,0:T(8,128)(2,1)S(1)} %shard_map.56.refs_0_), channel_id=1, source_target_pairs={{0,2},{2,0},{4,6},{6,4},{8,10},{10,8},{12,14},{14,12},{16,18},{18,... | collective-permute-start | bytes 2359304 | tf_op jit(solution)/shard_map/L_CM2a/ppermute | solution.py:280
  105.9 12.2 %collective-permute-start.26 = (bf16[384,1024]{1,0:T(8,128)(2,1)}, bf16[384,1024]{1,0:T(8,128)(2,1)S(1)}, u32[]{:S(2)}, u32[]{:S(2)}) collective-permute-start(bf16[384,1024]{1,0:T(8,128)(2,1)} %collective-permute-done.refs_0_), channel_id=1, source_target_pairs={{0,2},{2,0},{4,6},{6,4},{8,10},{10,8},{12,14},{14,12},{16,18},{18,... | collective-permute-start | bytes 2359304 | tf_op jit(solution)/shard_map/L_CPa/ppermute | solution.py:280
  117.5 6.2 %collective-permute-start.27 = (bf16[384,1024]{1,0:T(8,128)(2,1)S(1)}, bf16[384,1024]{1,0:T(8,128)(2,1)S(1)}, u32[]{:S(2)}, u32[]{:S(2)}) collective-permute-start(bf16[384,1024]{1,0:T(8,128)(2,1)S(1)} %collective-permute-done.22.refs_2_), channel_id=1, source_target_pairs={{0,2},{2,0},{4,6},{6,4},{8,10},{10,8},{12,14},{14,12},{16,18},{18,... | collective-permute-start | bytes 2359304 | tf_op jit(solution)/shard_map/L_CXM2a/ppermute | solution.py:280
  117.5 12.7 %collective-permute-start.21 = (bf16[384,1024]{1,0:T(8,128)(2,1)S(1)}, bf16[384,1024]{1,0:T(8,128)(2,1)S(1)}, u32[]{:S(2)}, u32[]{:S(2)}) collective-permute-start(bf16[384,1024]{1,0:T(8,128)(2,1)S(1)} %collective-permute-done.15.refs_2_), channel_id=1, source_target_pairs={{0,2},{2,0},{4,6},{6,4},{8,10},{10,8},{12,14},{14,12},{16,18},{18,... | collective-permute-start | bytes 2359304 | tf_op jit(solution)/shard_map/L_CXM1b/ppermute | solution.py:280
  118.0 13.7 %collective-permute-start.23 = (bf16[384,1024]{1,0:T(8,128)(2,1)}, bf16[384,1024]{1,0:T(8,128)(2,1)S(1)}, u32[]{:S(2)}, u32[]{:S(2)}) collective-permute-start(bf16[384,1024]{1,0:T(8,128)(2,1)} %collective-permute-done.2.refs_1_), channel_id=1, source_target_pairs={{0,2},{2,0},{4,6},{6,4},{8,10},{10,8},{12,14},{14,12},{16,18},{18,... | collective-permute-start | bytes 2359304 | tf_op jit(solution)/shard_map/L_CPb/ppermute | solution.py:280
  118.1 13.6 %collective-permute-start.24 = (bf16[384,1024]{1,0:T(8,128)(2,1)S(1)}, bf16[384,1024]{1,0:T(8,128)(2,1)S(1)}, u32[]{:S(2)}, u32[]{:S(2)}) collective-permute-start(bf16[384,1024]{1,0:T(8,128)(2,1)S(1)} %shard_map.60.refs_2_), channel_id=1, source_target_pairs={{0,2},{2,0},{4,6},{6,4},{8,10},{10,8},{12,14},{14,12},{16,18},{18,... | collective-permute-start | bytes 2359304 | tf_op jit(solution)/shard_map/L_CM2b/ppermute | solution.py:280
  118.6 22.8 %collective-permute-start.20 = (bf16[384,1024]{1,0:T(8,128)(2,1)S(1)}, bf16[384,1024]{1,0:T(8,128)(2,1)S(1)}, u32[]{:S(2)}, u32[]{:S(2)}) collective-permute-start(bf16[384,1024]{1,0:T(8,128)(2,1)S(1)} %slice.11), channel_id=1, source_target_pairs={{0,8},{2,10},{4,12},{6,14},{8,0},{10,2},{12,4},{14,6},{16,24},{18,... | collective-permute-start | bytes 2359304 | tf_op jit(solution)/shard_map/L_E/ppermute | solution.py:280
  123.6 19.3 %collective-permute-start.19 = (bf16[384,1024]{1,0:T(8,128)(2,1)S(1)}, bf16[384,1024]{1,0:T(8,128)(2,1)S(1)}, u32[]{:S(2)}, u32[]{:S(2)}) collective-permute-start(bf16[384,1024]{1,0:T(8,128)(2,1)S(1)} %shard_map.60.refs_2_), channel_id=1, source_target_pairs={{0,4},{2,6},{4,0},{6,2},{8,12},{10,14},{12,8},{14,10},{16,20},{18,... | collective-permute-start | bytes 2359304 | tf_op jit(solution)/shard_map/L_XM2b/ppermute | solution.py:280
  130.2 12.7 %collective-permute-start.28 = (bf16[2,192,512]{2,1,0:T(8,128)(2,1)S(1)}, bf16[2,192,512]{2,1,0:T(8,128)(2,1)S(1)}, u32[]{:S(2)}, u32[]{:S(2)}) collective-permute-start(bf16[2,192,512]{2,1,0:T(8,128)(2,1)S(1)} %shard_map.62), channel_id=1, source_target_pairs={{0,1},{1,0},{2,3},{3,2},{4,5},{5,4},{6,7},{7,6},{8,9},{9,8},{10,11... | collective-permute-start | bytes 1179656 | tf_op jit(solution)/shard_map/L_partial/ppermute | solution.py:367
  142.9 2.4 %collective-permute-start.29 = (bf16[384,1024]{1,0:T(8,128)(2,1)S(1)}, bf16[384,1024]{1,0:T(8,128)(2,1)S(1)}, u32[]{:S(2)}, u32[]{:S(2)}) collective-permute-start(bf16[384,1024]{1,0:T(8,128)(2,1)S(1)} %collective-permute-done.19.refs_0_), channel_id=1, source_target_pairs={{0,2},{2,0},{4,6},{6,4},{8,10},{10,8},{12,14},{14,12},{16,18},{18,... | collective-permute-start | bytes 2359304 | tf_op jit(solution)/shard_map/L_CXM2b/ppermute | solution.py:280
  142.9 3.4 %collective-permute-start.30 = (bf16[384,1024]{1,0:T(8,128)(2,1)S(1)}, bf16[384,1024]{1,0:T(8,128)(2,1)S(1)}, u32[]{:S(2)}, u32[]{:S(2)}) collective-permute-start(bf16[384,1024]{1,0:T(8,128)(2,1)S(1)} %collective-permute-done.20.refs_1_), channel_id=1, source_target_pairs={{0,2},{2,0},{4,6},{6,4},{8,10},{10,8},{12,14},{14,12},{16,18},{18,... | collective-permute-start | bytes 2359304 | tf_op jit(solution)/shard_map/L_CE/ppermute | solution.py:280

commit v3 on v2

--- a/solution.py
+++ b/solution.py
@@ -28,6 +28,7 @@
 def phase_panels(slab, beam_hkl):
     _, depth, columns = slab.shape
     w = columns // 2
+    block = depth // 2 if depth % 256 == 0 else depth
 
     def kernel(slab_ref, hkl_ref, whole_ref, first_ref, second_ref):
         col = lax.axis_index("col")
@@ -55,7 +56,12 @@
     return pl.pallas_call(
         kernel,
         out_shape=[jax.ShapeDtypeStruct((n * columns, depth), jnp.bfloat16) for n in (2, 1, 1)],
-        out_specs=[IN_VMEM] * 3,
+        grid=(depth // block,),
+        in_specs=[
+            pl.BlockSpec((2, block, columns), lambda i: (0, i, 0)),
+            pl.BlockSpec((3, block), lambda i: (0, i)),
+        ],
+        out_specs=[pl.BlockSpec((n * columns, block), lambda i: (0, i)) for n in (2, 1, 1)],
         compiler_params=pltpu.CompilerParams(vmem_limit_bytes=60 * 2**20),
         cost_estimate=pl.CostEstimate(flops=1000, bytes_accessed=1000, transcendentals=0),
     )(slab, beam_hkl)

time: 149 us -> 149 us (level)
  transfers between devices with their start and end apart: 31 -> 31, of which waited for: 11 -> 11; matrix products, arithmetic and copies ran while one was open for 1% -> 1% of each run, Pallas kernels for 38% -> 39%
where the time goes in v3:
time: 149 us; the launch traced here: 148 us
  Pallas kernels  63.3 us (42%)
  starting transfers between devices  48.1 us (32%)
  waiting for transfers between devices  33.6 us (23%)
  local copies, waits for them, and re-layouts  2.72 us (2%)
    pallas_call x9, Pallas kernels, multiply(): pl.pallas_call(kernel, out_shape=out_shape, in_specs=[pl.BlockSpec(memory...  46.7 us
    ppermute x30, starting transfers between devices, send(): return lax.ppermute(value, 'row', route)  46.5 us
    ppermute x30, waiting for transfers between devices, send(): return lax.ppermute(value, 'row', route)  33.6 us
    pallas_call x2, Pallas kernels, multiply_tiles(): pl.pallas_call(kernel, out_shape=out_shape, in_specs=[IN_VMEM] * (1 + cou...  4.52 us
    pallas_call x1, Pallas kernels, take(): pl.pallas_call(kernel, out_shape=jax.ShapeDtypeStruct((len(which), 2, row...  4.07 us
    pallas_call x1, Pallas kernels, phase_panels(): pl.pallas_call(kernel, out_shape=[jax.ShapeDtypeStruct((n * columns, dept...  3.67 us
  transfers between devices with their start and end apart: 31, of which 11 were waited for; matrix products, arithmetic and copies ran while one was open for 1% of the time, Pallas kernels for 39%

profile of v3, /device:TPU:0, one launch (start us, length us, event | category | flops | bytes accessed | tf_op | source)
XLA Modules:
  0.0 148.1 jit_solution(12181092662271352036)
XLA Ops:
  0.0 3.7 %shard_map.46 = (bf16[768,1024]{1,0:T(8,128)(2,1)}, bf16[384,1024]{1,0:T(8,128)(2,1)}, bf16[384,1024]{1,0:T(8,128)(2,1)}) custom-call(bf16[2,1024,384]{2,1,0:T(8,128)(2,1)} %slab_ref.1, s32[3,1024]{1,0:T(4,128)} %hkl_ref.1), custom_call_target="tpu_custom_call" | custom-call | flops 1000 | bytes 1000 | tf_op jit(solution)/shard_map/pallas_call | solution.py:56
  4.1 1.6 %collective-permute-start.1 = (bf16[384,1024]{1,0:T(8,128)(2,1)}, bf16[384,1024]{1,0:T(8,128)(2,1)}, u32[]{:S(2)}, u32[]{:S(2)}) collective-permute-start(bf16[384,1024]{1,0:T(8,128)(2,1)} %get-tuple-element.42), channel_id=1, source_target_pairs={{8,16},{10,18},{12,20},{14,22},{16,8},{18,10},{20,12},{22,14},{9,1... | collective-permute-start | bytes 2359304 | tf_op jit(solution)/shard_map/L_Qa/ppermute | solution.py:286
  5.7 2.5 %collective-permute-start.4 = (bf16[768,1024]{1,0:T(8,128)(2,1)}, bf16[768,1024]{1,0:T(8,128)(2,1)S(1)}, u32[]{:S(2)}, u32[]{:S(2)}) collective-permute-start(bf16[768,1024]{1,0:T(8,128)(2,1)} %get-tuple-element.45.refs_0_), channel_id=1, source_target_pairs={{0,4},{2,6},{4,0},{6,2},{8,12},{10,14},{12,8},{14,10},{16,20},{18,... | collective-permute-start | bytes 4718600 | tf_op jit(solution)/shard_map/L_XO/ppermute | solution.py:286
  8.2 3.5 %collective-permute-start = (bf16[384,1024]{1,0:T(8,128)(2,1)}, bf16[384,1024]{1,0:T(8,128)(2,1)}, u32[]{:S(2)}, u32[]{:S(2)}) collective-permute-start(bf16[384,1024]{1,0:T(8,128)(2,1)} %get-tuple-element.42), channel_id=1, source_target_pairs={{0,8},{2,10},{4,12},{6,14},{8,0},{10,2},{12,4},{14,6},{16,24},{18,... | collective-permute-start | bytes 2359304 | tf_op jit(solution)/shard_map/L_Pa/ppermute | solution.py:286
  11.7 1.6 %collective-permute-start.3 = (bf16[384,1024]{1,0:T(8,128)(2,1)}, bf16[384,1024]{1,0:T(8,128)(2,1)}, u32[]{:S(2)}, u32[]{:S(2)}) collective-permute-start(bf16[384,1024]{1,0:T(8,128)(2,1)} %get-tuple-element.44), channel_id=1, source_target_pairs={{8,16},{10,18},{12,20},{14,22},{16,8},{18,10},{20,12},{22,14},{9,1... | collective-permute-start | bytes 2359304 | tf_op jit(solution)/shard_map/L_Qb/ppermute | solution.py:286
  13.3 15.9 %collective-permute-start.2 = (bf16[384,1024]{1,0:T(8,128)(2,1)}, bf16[384,1024]{1,0:T(8,128)(2,1)}, u32[]{:S(2)}, u32[]{:S(2)}) collective-permute-start(bf16[384,1024]{1,0:T(8,128)(2,1)} %get-tuple-element.44), channel_id=1, source_target_pairs={{0,8},{2,10},{4,12},{6,14},{8,0},{10,2},{12,4},{14,6},{16,24},{18,... | collective-permute-start | bytes 2359304 | tf_op jit(solution)/shard_map/L_Pb/ppermute | solution.py:286
  29.2 0.7 fusion
  29.9 0.7 collective-permute-start.7
  30.7 1.3 collective-permute-start.6
  32.0 1.4 copy-done
  33.4 5.9 %shard_map.47.refs_2_ = f32[768,1024]{1,0:T(8,128)S(1)} custom-call(s32[17]{0:T(128)S(1)} %get-tuple-element.64.blocks_ref, bf16[2,512,16384]{2,1,0:T(8,128)(2,1)} %s_ref.19, bf16[768,1024]{1,0:T(8,128)(2,1)S(1)} %copy-done, bf16[768,1024]{1,0:T(8,128)(2,1)S(1)} %collective-permute-done.5.refs_1_), custom_call_target="tpu_custom_call" | custom-call | flops 1000 | bytes 1000 | tf_op jit(solution)/shard_map/pallas_call | solution.py:134
  39.3 8.7 %collective-permute-done.2.refs_1_ = bf16[384,1024]{1,0:T(8,128)(2,1)} collective-permute-done((bf16[384,1024]{1,0:T(8,128)(2,1)}, bf16[384,1024]{1,0:T(8,128)(2,1)}, u32[]{:S(2)}, u32[]{:S(2)}) %collective-permute-start.2) | collective-permute-done | bytes 786464 | tf_op jit(solution)/shard_map/L_Pb/ppermute | solution.py:286
  48.0 1.5 %collective-permute-start.8 = (bf16[384,1024]{1,0:T(8,128)(2,1)}, bf16[384,1024]{1,0:T(8,128)(2,1)S(1)}, u32[]{:S(2)}, u32[]{:S(2)}) collective-permute-start(bf16[384,1024]{1,0:T(8,128)(2,1)} %collective-permute-done.refs_0_), channel_id=1, source_target_pairs={{0,4},{2,6},{4,0},{6,2},{8,12},{10,14},{12,8},{14,10},{16,20},{18,... | collective-permute-start | bytes 2359304 | tf_op jit(solution)/shard_map/L_XPa/ppermute | solution.py:286
  50.1 1.3 collective-permute-start.12
  51.4 1.4 shard_map.48.refs_0_
  52.8 6.0 %shard_map.49.refs_1_ = f32[768,1024]{1,0:T(8,128)S(1)} custom-call(s32[17]{0:T(128)S(1)} %get-tuple-element.64.blocks_ref, bf16[2,512,16384]{2,1,0:T(8,128)(2,1)} %s_ref.19, bf16[768,1024]{1,0:T(8,128)(2,1)S(1)} %shard_map.48.refs_0_, bf16[768,1024]{1,0:T(8,128)(2,1)S(1)} %collective-permute-done.4.refs_1_, ...), custom_call_target="tpu_custom_call", output_to_operand_aliasing={{}: (4, {})} | custom-call | flops 1000 | bytes 1000 | tf_op jit(solution)/shard_map/pallas_call | solution.py:134
  58.8 6.0 %collective-permute-done.6.second_ref = bf16[384,1024]{1,0:T(8,128)(2,1)S(1)} collective-permute-done((bf16[384,1024]{1,0:T(8,128)(2,1)}, bf16[384,1024]{1,0:T(8,128)(2,1)S(1)}, u32[]{:S(2)}, u32[]{:S(2)}) %collective-permute-start.6) | collective-permute-done | bytes 786464 | tf_op jit(solution)/shard_map/L_Sa/ppermute | solution.py:286
  65.0 0.7 shard_map.50.refs_1_
  65.6 1.6 %collective-permute-start.13 = (bf16[384,1024]{1,0:T(8,128)(2,1)S(1)}, bf16[384,1024]{1,0:T(8,128)(2,1)S(1)}, u32[]{:S(2)}, u32[]{:S(2)}) collective-permute-start(bf16[384,1024]{1,0:T(8,128)(2,1)S(1)} %shard_map.50.refs_1_), channel_id=1, source_target_pairs={{0,4},{2,6},{4,0},{6,2},{8,12},{10,14},{12,8},{14,10},{16,20},{18,... | collective-permute-start | bytes 2359304 | tf_op jit(solution)/shard_map/L_XM1a/ppermute | solution.py:286
  67.4 0.7 collective-permute-start.9
  68.1 3.9 %shard_map.51.refs_2_.refs_3_ = f32[768,1024]{1,0:T(8,128)S(1)} custom-call(s32[17]{0:T(128)S(1)} %get-tuple-element.64.blocks_ref, bf16[2,512,16384]{2,1,0:T(8,128)(2,1)} %s_ref.19, bf16[768,1024]{1,0:T(8,128)(2,1)S(1)} %collective-permute-done.14.refs_0_, f32[768,1024]{1,0:T(8,128)S(1)} %shard_map.49.refs_1_), custom_call_target="tpu_custom_call", output_to_operand_aliasing={{}: (3, {})} | custom-call | flops 1000 | bytes 1000 | tf_op jit(solution)/shard_map/pallas_call | solution.py:134
  72.1 1.3 collective-permute-start.11
  73.4 4.1 %shard_map.52.refs_3_ = f32[384,1024]{1,0:T(8,128)S(1)} custom-call(s32[17]{0:T(128)S(1)} %get-tuple-element.64.blocks_ref, bf16[2,512,16384]{2,1,0:T(8,128)(2,1)} %s_ref.19, bf16[384,1024]{1,0:T(8,128)(2,1)S(1)} %collective-permute-done.8.refs_0_, bf16[384,1024]{1,0:T(8,128)(2,1)S(1)} %shard_map.50.refs_1_, f32[768,1024]{1,0:T(8,128)S(1)} %shard_map.51.refs_2_.refs_3_), custom_call_target="tpu_custom_call" | custom-call | flops 1000 | bytes 1000 | tf_op jit(solution)/shard_map/pallas_call | solution.py:134
  77.5 3.1 %collective-permute-done.12.second_ref = bf16[384,1024]{1,0:T(8,128)(2,1)S(1)} collective-permute-done((bf16[384,1024]{1,0:T(8,128)(2,1)}, bf16[384,1024]{1,0:T(8,128)(2,1)S(1)}, u32[]{:S(2)}, u32[]{:S(2)}) %collective-permute-start.12) | collective-permute-done | bytes 786464 | tf_op jit(solution)/shard_map/L_Sb/ppermute | solution.py:286
  80.6 1.7 %collective-permute-done.13.refs_2_ = bf16[384,1024]{1,0:T(8,128)(2,1)S(1)} collective-permute-done((bf16[384,1024]{1,0:T(8,128)(2,1)S(1)}, bf16[384,1024]{1,0:T(8,128)(2,1)S(1)}, u32[]{:S(2)}, u32[]{:S(2)}) %collective-permute-start.13) | collective-permute-done | bytes 786464 | tf_op jit(solution)/shard_map/L_XM1a/ppermute | solution.py:286
  82.3 0.7 shard_map.53.refs_0_
  82.9 1.6 %collective-permute-start.15 = (bf16[384,1024]{1,0:T(8,128)(2,1)S(1)}, bf16[384,1024]{1,0:T(8,128)(2,1)S(1)}, u32[]{:S(2)}, u32[]{:S(2)}) collective-permute-start(bf16[384,1024]{1,0:T(8,128)(2,1)S(1)} %shard_map.53.refs_0_), channel_id=1, source_target_pairs={{0,4},{2,6},{4,0},{6,2},{8,12},{10,14},{12,8},{14,10},{16,20},{18,... | collective-permute-start | bytes 2359304 | tf_op jit(solution)/shard_map/L_XM1b/ppermute | solution.py:286
  85.0 1.5 collective-permute-start.10
  86.5 5.2 %shard_map.55.refs_2_ = f32[384,1024]{1,0:T(8,128)S(1)} custom-call(s32[17]{0:T(128)S(1)} %get-tuple-element.64.blocks_ref, bf16[2,512,16384]{2,1,0:T(8,128)(2,1)} %s_ref.19, bf16[768,1024]{1,0:T(8,128)(2,1)S(1)} %collective-permute-done.16.refs_0_.refs_1_, ...), custom_call_target="tpu_custom_call", output_to_operand_aliasing={{}: (5, {})} | custom-call | flops 1000 | bytes 1000 | tf_op jit(solution)/shard_map/pallas_call | solution.py:134
  91.7 5.8 %collective-permute-done.11.second_ref = bf16[384,1024]{1,0:T(8,128)(2,1)S(1)} collective-permute-done((bf16[384,1024]{1,0:T(8,128)(2,1)S(1)}, bf16[384,1024]{1,0:T(8,128)(2,1)S(1)}, u32[]{:S(2)}, u32[]{:S(2)}) %collective-permute-start.11) | collective-permute-done | bytes 786464 | tf_op jit(solution)/shard_map/L_Ua/ppermute | solution.py:286
  97.4 1.7 %collective-permute-done.15.refs_2_ = bf16[384,1024]{1,0:T(8,128)(2,1)S(1)} collective-permute-done((bf16[384,1024]{1,0:T(8,128)(2,1)S(1)}, bf16[384,1024]{1,0:T(8,128)(2,1)S(1)}, u32[]{:S(2)}, u32[]{:S(2)}) %collective-permute-start.15) | collective-permute-done | bytes 786464 | tf_op jit(solution)/shard_map/L_XM1b/ppermute | solution.py:286
  99.1 0.7 shard_map.56.refs_0_
  99.8 1.6 %collective-permute-start.22 = (bf16[384,1024]{1,0:T(8,128)(2,1)S(1)}, bf16[384,1024]{1,0:T(8,128)(2,1)S(1)}, u32[]{:S(2)}, u32[]{:S(2)}) collective-permute-start(bf16[384,1024]{1,0:T(8,128)(2,1)S(1)} %shard_map.56.refs_0_), channel_id=1, source_target_pairs={{0,4},{2,6},{4,0},{6,2},{8,12},{10,14},{12,8},{14,10},{16,20},{18,... | collective-permute-start | bytes 2359304 | tf_op jit(solution)/shard_map/L_XM2a/ppermute | solution.py:286
  101.3 4.1 %shard_map.59.tiles_ref = bf16[4,2,512,1024]{3,2,1,0:T(8,128)(2,1)S(1)} custom-call(s32[17]{0:T(128)S(1)} %get-tuple-element.64.blocks_ref, bf16[2,512,16384]{2,1,0:T(8,128)(2,1)} %s_ref.19), custom_call_target="tpu_custom_call" | custom-call | flops 1000 | bytes 1000 | tf_op jit(solution)/shard_map/pallas_call | solution.py:160
  106.0 4.2 %shard_map.57.refs_4_ = f32[384,1024]{1,0:T(8,128)S(1)} custom-call(s32[17]{0:T(128)S(1)} %get-tuple-element.64.blocks_ref, bf16[2,512,16384]{2,1,0:T(8,128)(2,1)} %s_ref.19, bf16[384,1024]{1,0:T(8,128)(2,1)S(1)} %shard_map.56.refs_0_, bf16[384,1024]{1,0:T(8,128)(2,1)S(1)} %collective-permute-done.17.refs_1_, ...), custom_call_target="tpu_custom_call", output_to_operand_aliasing={{}: (4, {})} | custom-call | flops 1000 | bytes 1000 | tf_op jit(solution)/shard_map/pallas_call | solution.py:134
  110.2 5.1 %shard_map.58.refs_4_ = f32[384,1024]{1,0:T(8,128)S(1)} custom-call(s32[17]{0:T(128)S(1)} %get-tuple-element.64.blocks_ref, bf16[2,512,16384]{2,1,0:T(8,128)(2,1)} %s_ref.19, bf16[384,1024]{1,0:T(8,128)(2,1)S(1)} %shard_map.53.refs_0_, bf16[384,1024]{1,0:T(8,128)(2,1)S(1)} %collective-permute-done.18.refs_1_, ...), custom_call_target="tpu_custom_call" | custom-call | flops 1000 | bytes 1000 | tf_op jit(solution)/shard_map/pallas_call | solution.py:134
  115.4 0.9 shard_map.60.refs_2_
  116.3 0.7 collective-permute-done.22.refs_2_
  118.1 4.7 %collective-permute-start.20 = (bf16[384,1024]{1,0:T(8,128)(2,1)S(1)}, bf16[384,1024]{1,0:T(8,128)(2,1)S(1)}, u32[]{:S(2)}, u32[]{:S(2)}) collective-permute-start(bf16[384,1024]{1,0:T(8,128)(2,1)S(1)} %slice.11), channel_id=1, source_target_pairs={{0,8},{2,10},{4,12},{6,14},{8,0},{10,2},{12,4},{14,6},{16,24},{18,... | collective-permute-start | bytes 2359304 | tf_op jit(solution)/shard_map/L_E/ppermute | solution.py:286
  122.8 0.7 collective-permute-start.19
  123.4 6.0 %shard_map.62 = bf16[2,192,512]{2,1,0:T(8,128)(2,1)S(1)} custom-call(s32[17]{0:T(128)S(1)} %get-tuple-element.64.blocks_ref, bf16[2,512,16384]{2,1,0:T(8,128)(2,1)} %s_ref.19, bf16[384,1024]{1,0:T(8,128)(2,1)S(1)} %collective-permute-done.25.refs_0_, bf16[384,1024]{1,0:T(8,128)(2,1)S(1)} %collective-permute-done.26.refs_1_, ...), custom_call_target="tpu_custom_call" | custom-call | flops 1000 | bytes 1000 | tf_op jit(solution)/shard_map/pallas_call | solution.py:134
  129.5 1.6 %collective-permute-start.28 = (bf16[2,192,512]{2,1,0:T(8,128)(2,1)S(1)}, bf16[2,192,512]{2,1,0:T(8,128)(2,1)S(1)}, u32[]{:S(2)}, u32[]{:S(2)}) collective-permute-start(bf16[2,192,512]{2,1,0:T(8,128)(2,1)S(1)} %shard_map.62), channel_id=1, source_target_pairs={{0,1},{1,0},{2,3},{3,2},{4,5},{5,4},{6,7},{7,6},{8,9},{9,8},{10,11... | collective-permute-start | bytes 1179656 | tf_op jit(solution)/shard_map/L_partial/ppermute | solution.py:373
  131.1 6.2 %shard_map.61.refs_2_ = f32[384,1024]{1,0:T(8,128)S(1)} custom-call(s32[17]{0:T(128)S(1)} %get-tuple-element.64.blocks_ref, bf16[2,512,16384]{2,1,0:T(8,128)(2,1)} %s_ref.19, bf16[384,1024]{1,0:T(8,128)(2,1)S(1)} %collective-permute-done.21.refs_0_, bf16[384,1024]{1,0:T(8,128)(2,1)S(1)} %collective-permute-done.23.refs_1_, ...), custom_call_target="tpu_custom_call", output_to_operand_aliasing={{}: (6, {})} | custom-call | flops 1000 | bytes 1000 | tf_op jit(solution)/shard_map/pallas_call | solution.py:134
  137.3 3.3 %collective-permute-done.20.refs_1_ = bf16[384,1024]{1,0:T(8,128)(2,1)S(1)} collective-permute-done((bf16[384,1024]{1,0:T(8,128)(2,1)S(1)}, bf16[384,1024]{1,0:T(8,128)(2,1)S(1)}, u32[]{:S(2)}, u32[]{:S(2)}) %collective-permute-start.20) | collective-permute-done | bytes 786464 | tf_op jit(solution)/shard_map/L_E/ppermute | solution.py:286
  140.6 1.5 collective-permute-done.19.refs_0_
  142.6 1.9 %shard_map.63.refs_2_ = f32[384,1024]{1,0:T(8,128)S(1)} custom-call(bf16[4,2,512,1024]{3,2,1,0:T(8,128)(2,1)S(1)} %shard_map.59.tiles_ref, bf16[384,1024]{1,0:T(8,128)(2,1)S(1)} %collective-permute-done.19.refs_0_, bf16[384,1024]{1,0:T(8,128)(2,1)S(1)} %collective-permute-done.20.refs_1_, ...), custom_call_target="tpu_custom_call", output_to_operand_aliasing={{}: (3, {})} | custom-call | flops 1000 | bytes 1000 | tf_op jit(solution)/shard_map/pallas_call | solution.py:208
  144.5 1.0 collective-permute-done.30.refs_1_
  145.5 2.6 %shard_map.64 = bf16[2,192,512]{2,1,0:T(8,128)(2,1)} custom-call(bf16[4,2,512,1024]{3,2,1,0:T(8,128)(2,1)S(1)} %shard_map.59.tiles_ref, bf16[384,1024]{1,0:T(8,128)(2,1)S(1)} %collective-permute-done.29.refs_0_, bf16[384,1024]{1,0:T(8,128)(2,1)S(1)} %collective-permute-done.30.refs_1_, f32[384,1024]{1,0:T(8,128)S(1)} %shard_map.63.refs_2_, ...), custom_call_target="tpu_custom_call" | custom-call | flops 1000 | bytes 1000 | tf_op jit(solution)/shard_map/pallas_call | solution.py:208
  (38 shorter events, 4.3 us)
Async XLA Ops:
  3.7 27.0 %collective-permute-start.5 = (bf16[768,1024]{1,0:T(8,128)(2,1)}, bf16[768,1024]{1,0:T(8,128)(2,1)S(1)}, u32[]{:S(2)}, u32[]{:S(2)}) collective-permute-start(bf16[768,1024]{1,0:T(8,128)(2,1)} %get-tuple-element.45.refs_0_), channel_id=1, source_target_pairs={{0,2},{2,0},{4,6},{6,4},{8,10},{10,8},{12,14},{14,12},{16,18},{18,... | collective-permute-start | bytes 4718600 | tf_op jit(solution)/shard_map/L_CO/ppermute | solution.py:286
  4.1 9.2 %collective-permute-start.1 = (bf16[384,1024]{1,0:T(8,128)(2,1)}, bf16[384,1024]{1,0:T(8,128)(2,1)}, u32[]{:S(2)}, u32[]{:S(2)}) collective-permute-start(bf16[384,1024]{1,0:T(8,128)(2,1)} %get-tuple-element.42), channel_id=1, source_target_pairs={{8,16},{10,18},{12,20},{14,22},{16,8},{18,10},{20,12},{22,14},{9,1... | collective-permute-start | bytes 2359304 | tf_op jit(solution)/shard_map/L_Qa/ppermute | solution.py:286
  5.7 42.3 %collective-permute-start.4 = (bf16[768,1024]{1,0:T(8,128)(2,1)}, bf16[768,1024]{1,0:T(8,128)(2,1)S(1)}, u32[]{:S(2)}, u32[]{:S(2)}) collective-permute-start(bf16[768,1024]{1,0:T(8,128)(2,1)} %get-tuple-element.45.refs_0_), channel_id=1, source_target_pairs={{0,4},{2,6},{4,0},{6,2},{8,12},{10,14},{12,8},{14,10},{16,20},{18,... | collective-permute-start | bytes 4718600 | tf_op jit(solution)/shard_map/L_XO/ppermute | solution.py:286
  8.2 21.7 %collective-permute-start = (bf16[384,1024]{1,0:T(8,128)(2,1)}, bf16[384,1024]{1,0:T(8,128)(2,1)}, u32[]{:S(2)}, u32[]{:S(2)}) collective-permute-start(bf16[384,1024]{1,0:T(8,128)(2,1)} %get-tuple-element.42), channel_id=1, source_target_pairs={{0,8},{2,10},{4,12},{6,14},{8,0},{10,2},{12,4},{14,6},{16,24},{18,... | collective-permute-start | bytes 2359304 | tf_op jit(solution)/shard_map/L_Pa/ppermute | solution.py:286
  11.7 27.5 %collective-permute-start.3 = (bf16[384,1024]{1,0:T(8,128)(2,1)}, bf16[384,1024]{1,0:T(8,128)(2,1)}, u32[]{:S(2)}, u32[]{:S(2)}) collective-permute-start(bf16[384,1024]{1,0:T(8,128)(2,1)} %get-tuple-element.44), channel_id=1, source_target_pairs={{8,16},{10,18},{12,20},{14,22},{16,8},{18,10},{20,12},{22,14},{9,1... | collective-permute-start | bytes 2359304 | tf_op jit(solution)/shard_map/L_Qb/ppermute | solution.py:286
  13.3 34.7 %collective-permute-start.2 = (bf16[384,1024]{1,0:T(8,128)(2,1)}, bf16[384,1024]{1,0:T(8,128)(2,1)}, u32[]{:S(2)}, u32[]{:S(2)}) collective-permute-start(bf16[384,1024]{1,0:T(8,128)(2,1)} %get-tuple-element.44), channel_id=1, source_target_pairs={{0,8},{2,10},{4,12},{6,14},{8,0},{10,2},{12,4},{14,6},{16,24},{18,... | collective-permute-start | bytes 2359304 | tf_op jit(solution)/shard_map/L_Pb/ppermute | solution.py:286
  29.9 28.8 %collective-permute-start.7 = (bf16[384,1024]{1,0:T(8,128)(2,1)}, bf16[384,1024]{1,0:T(8,128)(2,1)S(1)}, u32[]{:S(2)}, u32[]{:S(2)}) collective-permute-start(bf16[384,1024]{1,0:T(8,128)(2,1)} %collective-permute-done.refs_0_), channel_id=1, source_target_pairs={{8,16},{10,18},{12,20},{14,22},{16,8},{18,10},{20,12},{22,14},{9,1... | collective-permute-start | bytes 2359304 | tf_op jit(solution)/shard_map/L_Ta/ppermute | solution.py:286
  30.7 34.1 %collective-permute-start.6 = (bf16[384,1024]{1,0:T(8,128)(2,1)}, bf16[384,1024]{1,0:T(8,128)(2,1)S(1)}, u32[]{:S(2)}, u32[]{:S(2)}) collective-permute-start(bf16[384,1024]{1,0:T(8,128)(2,1)} %collective-permute-done.1.first_ref), channel_id=1, source_target_pairs={{8,0},{10,2},{12,4},{14,6},{16,24},{18,26},{20,28},{22,30},{9,1},{... | collective-permute-start | bytes 2359304 | tf_op jit(solution)/shard_map/L_Sa/ppermute | solution.py:286
  32.0 1.4 copy-start
  48.0 17.0 %collective-permute-start.8 = (bf16[384,1024]{1,0:T(8,128)(2,1)}, bf16[384,1024]{1,0:T(8,128)(2,1)S(1)}, u32[]{:S(2)}, u32[]{:S(2)}) collective-permute-start(bf16[384,1024]{1,0:T(8,128)(2,1)} %collective-permute-done.refs_0_), channel_id=1, source_target_pairs={{0,4},{2,6},{4,0},{6,2},{8,12},{10,14},{12,8},{14,10},{16,20},{18,... | collective-permute-start | bytes 2359304 | tf_op jit(solution)/shard_map/L_XPa/ppermute | solution.py:286
  49.5 18.7 %collective-permute-start.14 = (bf16[768,1024]{1,0:T(8,128)(2,1)S(1)}, bf16[768,1024]{1,0:T(8,128)(2,1)S(1)}, u32[]{:S(2)}, u32[]{:S(2)}) collective-permute-start(bf16[768,1024]{1,0:T(8,128)(2,1)S(1)} %collective-permute-done.4.refs_1_), channel_id=1, source_target_pairs={{0,2},{2,0},{4,6},{6,4},{8,10},{10,8},{12,14},{14,12},{16,18},{18,... | collective-permute-start | bytes 4718600 | tf_op jit(solution)/shard_map/L_CXO/ppermute | solution.py:286
  50.1 30.5 %collective-permute-start.12 = (bf16[384,1024]{1,0:T(8,128)(2,1)}, bf16[384,1024]{1,0:T(8,128)(2,1)S(1)}, u32[]{:S(2)}, u32[]{:S(2)}) collective-permute-start(bf16[384,1024]{1,0:T(8,128)(2,1)} %collective-permute-done.3.first_ref), channel_id=1, source_target_pairs={{8,0},{10,2},{12,4},{14,6},{16,24},{18,26},{20,28},{22,30},{9,1},{... | collective-permute-start | bytes 2359304 | tf_op jit(solution)/shard_map/L_Sb/ppermute | solution.py:286
  65.6 16.6 %collective-permute-start.13 = (bf16[384,1024]{1,0:T(8,128)(2,1)S(1)}, bf16[384,1024]{1,0:T(8,128)(2,1)S(1)}, u32[]{:S(2)}, u32[]{:S(2)}) collective-permute-start(bf16[384,1024]{1,0:T(8,128)(2,1)S(1)} %shard_map.50.refs_1_), channel_id=1, source_target_pairs={{0,4},{2,6},{4,0},{6,2},{8,12},{10,14},{12,8},{14,10},{16,20},{18,... | collective-permute-start | bytes 2359304 | tf_op jit(solution)/shard_map/L_XM1a/ppermute | solution.py:286
  67.3 17.7 %collective-permute-start.16 = (bf16[768,1024]{1,0:T(8,128)(2,1)S(1)}, bf16[768,1024]{1,0:T(8,128)(2,1)S(1)}, u32[]{:S(2)}, u32[]{:S(2)}) collective-permute-start(bf16[768,1024]{1,0:T(8,128)(2,1)S(1)} %shard_map.54), channel_id=1, source_target_pairs={{0,2},{2,0},{4,6},{6,4},{8,10},{10,8},{12,14},{14,12},{16,18},{18,... | collective-permute-start | bytes 4718600 | tf_op jit(solution)/shard_map/L_CXPaM1a/ppermute | solution.py:286
  67.4 17.1 %collective-permute-start.9 = (bf16[384,1024]{1,0:T(8,128)(2,1)}, bf16[384,1024]{1,0:T(8,128)(2,1)S(1)}, u32[]{:S(2)}, u32[]{:S(2)}) collective-permute-start(bf16[384,1024]{1,0:T(8,128)(2,1)} %collective-permute-done.2.refs_1_), channel_id=1, source_target_pairs={{8,16},{10,18},{12,20},{14,22},{16,8},{18,10},{20,12},{22,14},{9,1... | collective-permute-start | bytes 2359304 | tf_op jit(solution)/shard_map/L_Tb/ppermute | solution.py:286
  72.1 25.4 %collective-permute-start.11 = (bf16[384,1024]{1,0:T(8,128)(2,1)S(1)}, bf16[384,1024]{1,0:T(8,128)(2,1)S(1)}, u32[]{:S(2)}, u32[]{:S(2)}) collective-permute-start(bf16[384,1024]{1,0:T(8,128)(2,1)S(1)} %collective-permute-done.7.first_ref), channel_id=1, source_target_pairs={{8,0},{10,2},{12,4},{14,6},{16,24},{18,26},{20,28},{22,30},{9,1},{... | collective-permute-start | bytes 2359304 | tf_op jit(solution)/shard_map/L_Ua/ppermute | solution.py:286
  82.9 16.2 %collective-permute-start.15 = (bf16[384,1024]{1,0:T(8,128)(2,1)S(1)}, bf16[384,1024]{1,0:T(8,128)(2,1)S(1)}, u32[]{:S(2)}, u32[]{:S(2)}) collective-permute-start(bf16[384,1024]{1,0:T(8,128)(2,1)S(1)} %shard_map.53.refs_0_), channel_id=1, source_target_pairs={{0,4},{2,6},{4,0},{6,2},{8,12},{10,14},{12,8},{14,10},{16,20},{18,... | collective-permute-start | bytes 2359304 | tf_op jit(solution)/shard_map/L_XM1b/ppermute | solution.py:286
  84.5 20.9 %collective-permute-start.17 = (bf16[384,1024]{1,0:T(8,128)(2,1)S(1)}, bf16[384,1024]{1,0:T(8,128)(2,1)S(1)}, u32[]{:S(2)}, u32[]{:S(2)}) collective-permute-start(bf16[384,1024]{1,0:T(8,128)(2,1)S(1)} %collective-permute-done.13.refs_2_), channel_id=1, source_target_pairs={{0,2},{2,0},{4,6},{6,4},{8,10},{10,8},{12,14},{14,12},{16,18},{18,... | collective-permute-start | bytes 2359304 | tf_op jit(solution)/shard_map/L_CXM1a/ppermute | solution.py:286
  84.5 25.7 %collective-permute-start.18 = (bf16[384,1024]{1,0:T(8,128)(2,1)S(1)}, bf16[384,1024]{1,0:T(8,128)(2,1)S(1)}, u32[]{:S(2)}, u32[]{:S(2)}) collective-permute-start(bf16[384,1024]{1,0:T(8,128)(2,1)S(1)} %shard_map.53.refs_0_), channel_id=1, source_target_pairs={{0,2},{2,0},{4,6},{6,4},{8,10},{10,8},{12,14},{14,12},{16,18},{18,... | collective-permute-start | bytes 2359304 | tf_op jit(solution)/shard_map/L_CM1b/ppermute | solution.py:286
  85.0 30.4 %collective-permute-start.10 = (bf16[384,1024]{1,0:T(8,128)(2,1)S(1)}, bf16[384,1024]{1,0:T(8,128)(2,1)S(1)}, u32[]{:S(2)}, u32[]{:S(2)}) collective-permute-start(bf16[384,1024]{1,0:T(8,128)(2,1)S(1)} %collective-permute-done.9.first_ref), channel_id=1, source_target_pairs={{8,0},{10,2},{12,4},{14,6},{16,24},{18,26},{20,28},{22,30},{9,1},{... | collective-permute-start | bytes 2359304 | tf_op jit(solution)/shard_map/L_Ub/ppermute | solution.py:286
  99.8 17.2 %collective-permute-start.22 = (bf16[384,1024]{1,0:T(8,128)(2,1)S(1)}, bf16[384,1024]{1,0:T(8,128)(2,1)S(1)}, u32[]{:S(2)}, u32[]{:S(2)}) collective-permute-start(bf16[384,1024]{1,0:T(8,128)(2,1)S(1)} %shard_map.56.refs_0_), channel_id=1, source_target_pairs={{0,4},{2,6},{4,0},{6,2},{8,12},{10,14},{12,8},{14,10},{16,20},{18,... | collective-permute-start | bytes 2359304 | tf_op jit(solution)/shard_map/L_XM2a/ppermute | solution.py:286
  101.3 16.8 %collective-permute-start.25 = (bf16[384,1024]{1,0:T(8,128)(2,1)S(1)}, bf16[384,1024]{1,0:T(8,128)(2,1)S(1)}, u32[]{:S(2)}, u32[]{:S(2)}) collective-permute-start(bf16[384,1024]{1,0:T(8,128)(2,1)S(1)} %shard_map.56.refs_0_), channel_id=1, source_target_pairs={{0,2},{2,0},{4,6},{6,4},{8,10},{10,8},{12,14},{14,12},{16,18},{18,... | collective-permute-start | bytes 2359304 | tf_op jit(solution)/shard_map/L_CM2a/ppermute | solution.py:286
  105.4 12.2 %collective-permute-start.26 = (bf16[384,1024]{1,0:T(8,128)(2,1)}, bf16[384,1024]{1,0:T(8,128)(2,1)S(1)}, u32[]{:S(2)}, u32[]{:S(2)}) collective-permute-start(bf16[384,1024]{1,0:T(8,128)(2,1)} %collective-permute-done.refs_0_), channel_id=1, source_target_pairs={{0,2},{2,0},{4,6},{6,4},{8,10},{10,8},{12,14},{14,12},{16,18},{18,... | collective-permute-start | bytes 2359304 | tf_op jit(solution)/shard_map/L_CPa/ppermute | solution.py:286
  117.0 5.8 %collective-permute-start.27 = (bf16[384,1024]{1,0:T(8,128)(2,1)S(1)}, bf16[384,1024]{1,0:T(8,128)(2,1)S(1)}, u32[]{:S(2)}, u32[]{:S(2)}) collective-permute-start(bf16[384,1024]{1,0:T(8,128)(2,1)S(1)} %collective-permute-done.22.refs_2_), channel_id=1, source_target_pairs={{0,2},{2,0},{4,6},{6,4},{8,10},{10,8},{12,14},{14,12},{16,18},{18,... | collective-permute-start | bytes 2359304 | tf_op jit(solution)/shard_map/L_CXM2a/ppermute | solution.py:286
  117.0 12.5 %collective-permute-start.21 = (bf16[384,1024]{1,0:T(8,128)(2,1)S(1)}, bf16[384,1024]{1,0:T(8,128)(2,1)S(1)}, u32[]{:S(2)}, u32[]{:S(2)}) collective-permute-start(bf16[384,1024]{1,0:T(8,128)(2,1)S(1)} %collective-permute-done.15.refs_2_), channel_id=1, source_target_pairs={{0,2},{2,0},{4,6},{6,4},{8,10},{10,8},{12,14},{14,12},{16,18},{18,... | collective-permute-start | bytes 2359304 | tf_op jit(solution)/shard_map/L_CXM1b/ppermute | solution.py:286
  117.5 13.6 %collective-permute-start.23 = (bf16[384,1024]{1,0:T(8,128)(2,1)}, bf16[384,1024]{1,0:T(8,128)(2,1)S(1)}, u32[]{:S(2)}, u32[]{:S(2)}) collective-permute-start(bf16[384,1024]{1,0:T(8,128)(2,1)} %collective-permute-done.2.refs_1_), channel_id=1, source_target_pairs={{0,2},{2,0},{4,6},{6,4},{8,10},{10,8},{12,14},{14,12},{16,18},{18,... | collective-permute-start | bytes 2359304 | tf_op jit(solution)/shard_map/L_CPb/ppermute | solution.py:286
  117.6 13.5 %collective-permute-start.24 = (bf16[384,1024]{1,0:T(8,128)(2,1)S(1)}, bf16[384,1024]{1,0:T(8,128)(2,1)S(1)}, u32[]{:S(2)}, u32[]{:S(2)}) collective-permute-start(bf16[384,1024]{1,0:T(8,128)(2,1)S(1)} %shard_map.60.refs_2_), channel_id=1, source_target_pairs={{0,2},{2,0},{4,6},{6,4},{8,10},{10,8},{12,14},{14,12},{16,18},{18,... | collective-permute-start | bytes 2359304 | tf_op jit(solution)/shard_map/L_CM2b/ppermute | solution.py:286
  118.1 22.5 %collective-permute-start.20 = (bf16[384,1024]{1,0:T(8,128)(2,1)S(1)}, bf16[384,1024]{1,0:T(8,128)(2,1)S(1)}, u32[]{:S(2)}, u32[]{:S(2)}) collective-permute-start(bf16[384,1024]{1,0:T(8,128)(2,1)S(1)} %slice.11), channel_id=1, source_target_pairs={{0,8},{2,10},{4,12},{6,14},{8,0},{10,2},{12,4},{14,6},{16,24},{18,... | collective-permute-start | bytes 2359304 | tf_op jit(solution)/shard_map/L_E/ppermute | solution.py:286
  122.8 19.3 %collective-permute-start.19 = (bf16[384,1024]{1,0:T(8,128)(2,1)S(1)}, bf16[384,1024]{1,0:T(8,128)(2,1)S(1)}, u32[]{:S(2)}, u32[]{:S(2)}) collective-permute-start(bf16[384,1024]{1,0:T(8,128)(2,1)S(1)} %shard_map.60.refs_2_), channel_id=1, source_target_pairs={{0,4},{2,6},{4,0},{6,2},{8,12},{10,14},{12,8},{14,10},{16,20},{18,... | collective-permute-start | bytes 2359304 | tf_op jit(solution)/shard_map/L_XM2b/ppermute | solution.py:286
  129.5 12.6 %collective-permute-start.28 = (bf16[2,192,512]{2,1,0:T(8,128)(2,1)S(1)}, bf16[2,192,512]{2,1,0:T(8,128)(2,1)S(1)}, u32[]{:S(2)}, u32[]{:S(2)}) collective-permute-start(bf16[2,192,512]{2,1,0:T(8,128)(2,1)S(1)} %shard_map.62), channel_id=1, source_target_pairs={{0,1},{1,0},{2,3},{3,2},{4,5},{5,4},{6,7},{7,6},{8,9},{9,8},{10,11... | collective-permute-start | bytes 1179656 | tf_op jit(solution)/shard_map/L_partial/ppermute | solution.py:373
  142.0 2.4 %collective-permute-start.29 = (bf16[384,1024]{1,0:T(8,128)(2,1)S(1)}, bf16[384,1024]{1,0:T(8,128)(2,1)S(1)}, u32[]{:S(2)}, u32[]{:S(2)}) collective-permute-start(bf16[384,1024]{1,0:T(8,128)(2,1)S(1)} %collective-permute-done.19.refs_0_), channel_id=1, source_target_pairs={{0,2},{2,0},{4,6},{6,4},{8,10},{10,8},{12,14},{14,12},{16,18},{18,... | collective-permute-start | bytes 2359304 | tf_op jit(solution)/shard_map/L_CXM2b/ppermute | solution.py:286
  142.0 3.4 %collective-permute-start.30 = (bf16[384,1024]{1,0:T(8,128)(2,1)S(1)}, bf16[384,1024]{1,0:T(8,128)(2,1)S(1)}, u32[]{:S(2)}, u32[]{:S(2)}) collective-permute-start(bf16[384,1024]{1,0:T(8,128)(2,1)S(1)} %collective-permute-done.20.refs_1_), channel_id=1, source_target_pairs={{0,2},{2,0},{4,6},{6,4},{8,10},{10,8},{12,14},{14,12},{16,18},{18,... | collective-permute-start | bytes 2359304 | tf_op jit(solution)/shard_map/L_CE/ppermute | solution.py:286

commit v4 on v3

--- a/solution.py
+++ b/solution.py
@@ -360,7 +360,6 @@
     E = send(XO[wide:], outer, "E")
     CXM1b, CM2a = C(XM1b, "XM1b"), C(M2a, "M2a")
     CPa = C(after(Pa, M2a), "Pa")
-    A = mul(["N", "xcM"], [M2a, CXM1a], A)
     B = mul(["M", "cM", "xM"], [M1b, CM1b, XM1b], b(AB))
     Ub, A, B, tiles = ob((Ub, A, B, tiles))
     M2b = choose(in_middle, Tb, Ub)
@@ -368,7 +367,7 @@
     XM2a, M2b = ob((XM2a, M2b))
     CXM2a, CM2b = C(XM2a, "XM2a"), C(M2b, "M2b")
     CPb = C(after(Pb, M2b), "Pb")
-    partial = mul(["cN", "cP", "xN", "xcN"], [CM2a, CPa, XM2a, CXM2a], A, finish=True)
+    partial = mul(["N", "xcM", "cN", "cP", "xN", "xcN"], [M2a, CXM1a, CM2a, CPa, XM2a, CXM2a], A, finish=True)
     with jax.named_scope("L_partial"):
         received = lax.ppermute(partial, "col", [(0, 1), (1, 0)])
     B = mul(["xcM", "cP", "N", "cN"], [CXM1b, CPb, M2b, CM2b], B)

time: 149 us -> 149 us (level)
  waiting for transfers between devices: 33.6 us -> 37 us
  Pallas kernels: 63.3 us -> 60.8 us
    ppermute x30, waiting for transfers between devices: 33.6 us -> 37 us  [send(): return lax.ppermute(value, 'row', route)]
    pallas_call x9 -> x8, Pallas kernels: 46.7 us -> 44.4 us  [multiply(): pl.pallas_call(kernel, out_shape=out_shape, in_specs=[pl.BlockSpec(memory...]
  transfers between devices with their start and end apart: 31 -> 31, of which waited for: 11 -> 12; matrix products, arithmetic and copies ran while one was open for 1% -> 1% of each run, Pallas kernels for 39% -> 37%
where the time goes in v4:
time: 149 us; the launch traced here: 148 us
  Pallas kernels  60.8 us (41%)
  starting transfers between devices  47.2 us (32%)
  waiting for transfers between devices  37 us (25%)
  local copies, waits for them, and re-layouts  2.72 us (2%)
    ppermute x30, starting transfers between devices, send(): return lax.ppermute(value, 'row', route)  45.7 us
    pallas_call x8, Pallas kernels, multiply(): pl.pallas_call(kernel, out_shape=out_shape, in_specs=[pl.BlockSpec(memory...  44.4 us
    ppermute x30, waiting for transfers between devices, send(): return lax.ppermute(value, 'row', route)  37 us
    pallas_call x2, Pallas kernels, multiply_tiles(): pl.pallas_call(kernel, out_shape=out_shape, in_specs=[IN_VMEM] * (1 + cou...  4.51 us
    pallas_call x1, Pallas kernels, take(): pl.pallas_call(kernel, out_shape=jax.ShapeDtypeStruct((len(which), 2, row...  4.07 us
    pallas_call x1, Pallas kernels, phase_panels(): pl.pallas_call(kernel, out_shape=[jax.ShapeDtypeStruct((n * columns, dept...  3.67 us
  transfers between devices with their start and end apart: 31, of which 12 were waited for; matrix products, arithmetic and copies ran while one was open for 1% of the time, Pallas kernels for 37%

profile of v4, /device:TPU:0, one launch (start us, length us, event | category | flops | bytes accessed | tf_op | source)
XLA Modules:
  0.0 148.1 jit_solution(16222369705766786848)
XLA Ops:
  0.0 3.7 %shard_map.46 = (bf16[768,1024]{1,0:T(8,128)(2,1)}, bf16[384,1024]{1,0:T(8,128)(2,1)}, bf16[384,1024]{1,0:T(8,128)(2,1)}) custom-call(bf16[2,1024,384]{2,1,0:T(8,128)(2,1)} %slab_ref.1, s32[3,1024]{1,0:T(4,128)} %hkl_ref.1), custom_call_target="tpu_custom_call" | custom-call | flops 1000 | bytes 1000 | tf_op jit(solution)/shard_map/pallas_call | solution.py:56
  4.1 1.6 %collective-permute-start.1 = (bf16[384,1024]{1,0:T(8,128)(2,1)}, bf16[384,1024]{1,0:T(8,128)(2,1)}, u32[]{:S(2)}, u32[]{:S(2)}) collective-permute-start(bf16[384,1024]{1,0:T(8,128)(2,1)} %get-tuple-element.42), channel_id=1, source_target_pairs={{8,16},{10,18},{12,20},{14,22},{16,8},{18,10},{20,12},{22,14},{9,1... | collective-permute-start | bytes 2359304 | tf_op jit(solution)/shard_map/L_Qa/ppermute | solution.py:286
  5.7 2.5 %collective-permute-start.4 = (bf16[768,1024]{1,0:T(8,128)(2,1)}, bf16[768,1024]{1,0:T(8,128)(2,1)S(1)}, u32[]{:S(2)}, u32[]{:S(2)}) collective-permute-start(bf16[768,1024]{1,0:T(8,128)(2,1)} %get-tuple-element.45.refs_0_), channel_id=1, source_target_pairs={{0,4},{2,6},{4,0},{6,2},{8,12},{10,14},{12,8},{14,10},{16,20},{18,... | collective-permute-start | bytes 4718600 | tf_op jit(solution)/shard_map/L_XO/ppermute | solution.py:286
  8.2 3.5 %collective-permute-start = (bf16[384,1024]{1,0:T(8,128)(2,1)}, bf16[384,1024]{1,0:T(8,128)(2,1)}, u32[]{:S(2)}, u32[]{:S(2)}) collective-permute-start(bf16[384,1024]{1,0:T(8,128)(2,1)} %get-tuple-element.42), channel_id=1, source_target_pairs={{0,8},{2,10},{4,12},{6,14},{8,0},{10,2},{12,4},{14,6},{16,24},{18,... | collective-permute-start | bytes 2359304 | tf_op jit(solution)/shard_map/L_Pa/ppermute | solution.py:286
  11.7 1.6 %collective-permute-start.3 = (bf16[384,1024]{1,0:T(8,128)(2,1)}, bf16[384,1024]{1,0:T(8,128)(2,1)}, u32[]{:S(2)}, u32[]{:S(2)}) collective-permute-start(bf16[384,1024]{1,0:T(8,128)(2,1)} %get-tuple-element.44), channel_id=1, source_target_pairs={{8,16},{10,18},{12,20},{14,22},{16,8},{18,10},{20,12},{22,14},{9,1... | collective-permute-start | bytes 2359304 | tf_op jit(solution)/shard_map/L_Qb/ppermute | solution.py:286
  13.3 15.9 %collective-permute-start.2 = (bf16[384,1024]{1,0:T(8,128)(2,1)}, bf16[384,1024]{1,0:T(8,128)(2,1)}, u32[]{:S(2)}, u32[]{:S(2)}) collective-permute-start(bf16[384,1024]{1,0:T(8,128)(2,1)} %get-tuple-element.44), channel_id=1, source_target_pairs={{0,8},{2,10},{4,12},{6,14},{8,0},{10,2},{12,4},{14,6},{16,24},{18,... | collective-permute-start | bytes 2359304 | tf_op jit(solution)/shard_map/L_Pb/ppermute | solution.py:286
  29.2 0.7 fusion
  29.9 0.7 collective-permute-start.7
  30.7 1.3 collective-permute-start.6
  32.0 1.4 copy-done
  33.4 5.9 %shard_map.47.refs_2_ = f32[768,1024]{1,0:T(8,128)S(1)} custom-call(s32[17]{0:T(128)S(1)} %get-tuple-element.63.blocks_ref, bf16[2,512,16384]{2,1,0:T(8,128)(2,1)} %s_ref.17, bf16[768,1024]{1,0:T(8,128)(2,1)S(1)} %copy-done, bf16[768,1024]{1,0:T(8,128)(2,1)S(1)} %collective-permute-done.5.refs_1_), custom_call_target="tpu_custom_call" | custom-call | flops 1000 | bytes 1000 | tf_op jit(solution)/shard_map/pallas_call | solution.py:134
  39.3 8.7 %collective-permute-done.2.refs_1_ = bf16[384,1024]{1,0:T(8,128)(2,1)} collective-permute-done((bf16[384,1024]{1,0:T(8,128)(2,1)}, bf16[384,1024]{1,0:T(8,128)(2,1)}, u32[]{:S(2)}, u32[]{:S(2)}) %collective-permute-start.2) | collective-permute-done | bytes 786464 | tf_op jit(solution)/shard_map/L_Pb/ppermute | solution.py:286
  48.0 1.5 %collective-permute-start.8 = (bf16[384,1024]{1,0:T(8,128)(2,1)}, bf16[384,1024]{1,0:T(8,128)(2,1)S(1)}, u32[]{:S(2)}, u32[]{:S(2)}) collective-permute-start(bf16[384,1024]{1,0:T(8,128)(2,1)} %collective-permute-done.refs_0_), channel_id=1, source_target_pairs={{0,4},{2,6},{4,0},{6,2},{8,12},{10,14},{12,8},{14,10},{16,20},{18,... | collective-permute-start | bytes 2359304 | tf_op jit(solution)/shard_map/L_XPa/ppermute | solution.py:286
  49.5 0.6 slice.9
  50.1 1.3 collective-permute-start.12
  51.4 1.4 shard_map.48.refs_0_
  52.8 6.0 %shard_map.49.refs_1_ = f32[768,1024]{1,0:T(8,128)S(1)} custom-call(s32[17]{0:T(128)S(1)} %get-tuple-element.63.blocks_ref, bf16[2,512,16384]{2,1,0:T(8,128)(2,1)} %s_ref.17, bf16[768,1024]{1,0:T(8,128)(2,1)S(1)} %shard_map.48.refs_0_, bf16[768,1024]{1,0:T(8,128)(2,1)S(1)} %collective-permute-done.4.refs_1_, ...), custom_call_target="tpu_custom_call", output_to_operand_aliasing={{}: (4, {})} | custom-call | flops 1000 | bytes 1000 | tf_op jit(solution)/shard_map/pallas_call | solution.py:134
  58.8 5.9 %collective-permute-done.6.second_ref = bf16[384,1024]{1,0:T(8,128)(2,1)S(1)} collective-permute-done((bf16[384,1024]{1,0:T(8,128)(2,1)}, bf16[384,1024]{1,0:T(8,128)(2,1)S(1)}, u32[]{:S(2)}, u32[]{:S(2)}) %collective-permute-start.6) | collective-permute-done | bytes 786464 | tf_op jit(solution)/shard_map/L_Sa/ppermute | solution.py:286
  65.0 0.7 shard_map.50.refs_1_
  65.6 1.6 %collective-permute-start.13 = (bf16[384,1024]{1,0:T(8,128)(2,1)S(1)}, bf16[384,1024]{1,0:T(8,128)(2,1)S(1)}, u32[]{:S(2)}, u32[]{:S(2)}) collective-permute-start(bf16[384,1024]{1,0:T(8,128)(2,1)S(1)} %shard_map.50.refs_1_), channel_id=1, source_target_pairs={{0,4},{2,6},{4,0},{6,2},{8,12},{10,14},{12,8},{14,10},{16,20},{18,... | collective-permute-start | bytes 2359304 | tf_op jit(solution)/shard_map/L_XM1a/ppermute | solution.py:286
  67.4 0.7 collective-permute-start.9
  68.1 3.9 %shard_map.51.refs_2_.refs_3_ = f32[768,1024]{1,0:T(8,128)S(1)} custom-call(s32[17]{0:T(128)S(1)} %get-tuple-element.63.blocks_ref, bf16[2,512,16384]{2,1,0:T(8,128)(2,1)} %s_ref.17, bf16[768,1024]{1,0:T(8,128)(2,1)S(1)} %collective-permute-done.14.refs_0_, f32[768,1024]{1,0:T(8,128)S(1)} %shard_map.49.refs_1_), custom_call_target="tpu_custom_call", output_to_operand_aliasing={{}: (3, {})} | custom-call | flops 1000 | bytes 1000 | tf_op jit(solution)/shard_map/pallas_call | solution.py:134
  72.1 1.3 collective-permute-start.11
  73.4 4.1 %shard_map.52.refs_3_ = f32[384,1024]{1,0:T(8,128)S(1)} custom-call(s32[17]{0:T(128)S(1)} %get-tuple-element.63.blocks_ref, bf16[2,512,16384]{2,1,0:T(8,128)(2,1)} %s_ref.17, bf16[384,1024]{1,0:T(8,128)(2,1)S(1)} %collective-permute-done.8.refs_0_, bf16[384,1024]{1,0:T(8,128)(2,1)S(1)} %shard_map.50.refs_1_, f32[768,1024]{1,0:T(8,128)S(1)} %shard_map.51.refs_2_.refs_3_), custom_call_target="tpu_custom_call" | custom-call | flops 1000 | bytes 1000 | tf_op jit(solution)/shard_map/pallas_call | solution.py:134
  77.5 3.1 %collective-permute-done.12.second_ref = bf16[384,1024]{1,0:T(8,128)(2,1)S(1)} collective-permute-done((bf16[384,1024]{1,0:T(8,128)(2,1)}, bf16[384,1024]{1,0:T(8,128)(2,1)S(1)}, u32[]{:S(2)}, u32[]{:S(2)}) %collective-permute-start.12) | collective-permute-done | bytes 786464 | tf_op jit(solution)/shard_map/L_Sb/ppermute | solution.py:286
  80.6 1.7 %collective-permute-done.13.refs_2_ = bf16[384,1024]{1,0:T(8,128)(2,1)S(1)} collective-permute-done((bf16[384,1024]{1,0:T(8,128)(2,1)S(1)}, bf16[384,1024]{1,0:T(8,128)(2,1)S(1)}, u32[]{:S(2)}, u32[]{:S(2)}) %collective-permute-start.13) | collective-permute-done | bytes 786464 | tf_op jit(solution)/shard_map/L_XM1a/ppermute | solution.py:286
  82.3 0.7 shard_map.53.refs_0_
  82.9 1.6 %collective-permute-start.15 = (bf16[384,1024]{1,0:T(8,128)(2,1)S(1)}, bf16[384,1024]{1,0:T(8,128)(2,1)S(1)}, u32[]{:S(2)}, u32[]{:S(2)}) collective-permute-start(bf16[384,1024]{1,0:T(8,128)(2,1)S(1)} %shard_map.53.refs_0_), channel_id=1, source_target_pairs={{0,4},{2,6},{4,0},{6,2},{8,12},{10,14},{12,8},{14,10},{16,20},{18,... | collective-permute-start | bytes 2359304 | tf_op jit(solution)/shard_map/L_XM1b/ppermute | solution.py:286
  84.5 1.5 collective-permute-start.10
  86.0 5.2 %shard_map.55.refs_6_ = f32[384,1024]{1,0:T(8,128)S(1)} custom-call(s32[17]{0:T(128)S(1)} %get-tuple-element.63.blocks_ref, bf16[2,512,16384]{2,1,0:T(8,128)(2,1)} %s_ref.17, bf16[768,1024]{1,0:T(8,128)(2,1)S(1)} %collective-permute-done.16.refs_0_.refs_1_, ...), custom_call_target="tpu_custom_call", output_to_operand_aliasing={{}: (5, {})} | custom-call | flops 1000 | bytes 1000 | tf_op jit(solution)/shard_map/pallas_call | solution.py:134
  91.2 6.3 %collective-permute-done.11.second_ref = bf16[384,1024]{1,0:T(8,128)(2,1)S(1)} collective-permute-done((bf16[384,1024]{1,0:T(8,128)(2,1)S(1)}, bf16[384,1024]{1,0:T(8,128)(2,1)S(1)}, u32[]{:S(2)}, u32[]{:S(2)}) %collective-permute-start.11) | collective-permute-done | bytes 786464 | tf_op jit(solution)/shard_map/L_Ua/ppermute | solution.py:286
  97.4 1.7 %collective-permute-done.15.refs_2_ = bf16[384,1024]{1,0:T(8,128)(2,1)S(1)} collective-permute-done((bf16[384,1024]{1,0:T(8,128)(2,1)S(1)}, bf16[384,1024]{1,0:T(8,128)(2,1)S(1)}, u32[]{:S(2)}, u32[]{:S(2)}) %collective-permute-start.15) | collective-permute-done | bytes 786464 | tf_op jit(solution)/shard_map/L_XM1b/ppermute | solution.py:286
  99.1 0.7 shard_map.59.refs_0_
  99.8 1.6 %collective-permute-start.21 = (bf16[384,1024]{1,0:T(8,128)(2,1)S(1)}, bf16[384,1024]{1,0:T(8,128)(2,1)S(1)}, u32[]{:S(2)}, u32[]{:S(2)}) collective-permute-start(bf16[384,1024]{1,0:T(8,128)(2,1)S(1)} %shard_map.59.refs_0_), channel_id=1, source_target_pairs={{0,4},{2,6},{4,0},{6,2},{8,12},{10,14},{12,8},{14,10},{16,20},{18,... | collective-permute-start | bytes 2359304 | tf_op jit(solution)/shard_map/L_XM2a/ppermute | solution.py:286
  101.8 4.1 %shard_map.57.tiles_ref = bf16[4,2,512,1024]{3,2,1,0:T(8,128)(2,1)S(1)} custom-call(s32[17]{0:T(128)S(1)} %get-tuple-element.63.blocks_ref, bf16[2,512,16384]{2,1,0:T(8,128)(2,1)} %s_ref.17), custom_call_target="tpu_custom_call" | custom-call | flops 1000 | bytes 1000 | tf_op jit(solution)/shard_map/pallas_call | solution.py:160
  106.0 5.1 %shard_map.56.refs_4_ = f32[384,1024]{1,0:T(8,128)S(1)} custom-call(s32[17]{0:T(128)S(1)} %get-tuple-element.63.blocks_ref, bf16[2,512,16384]{2,1,0:T(8,128)(2,1)} %s_ref.17, bf16[384,1024]{1,0:T(8,128)(2,1)S(1)} %shard_map.53.refs_0_, bf16[384,1024]{1,0:T(8,128)(2,1)S(1)} %collective-permute-done.17.refs_1_, ...), custom_call_target="tpu_custom_call" | custom-call | flops 1000 | bytes 1000 | tf_op jit(solution)/shard_map/pallas_call | solution.py:134
  111.1 2.8 %collective-permute-done.10.second_ref = bf16[384,1024]{1,0:T(8,128)(2,1)S(1)} collective-permute-done((bf16[384,1024]{1,0:T(8,128)(2,1)S(1)}, bf16[384,1024]{1,0:T(8,128)(2,1)S(1)}, u32[]{:S(2)}, u32[]{:S(2)}) %collective-permute-start.10) | collective-permute-done | bytes 786464 | tf_op jit(solution)/shard_map/L_Ub/ppermute | solution.py:286
  113.9 0.7 shard_map.58.refs_2_
  114.6 2.4 %collective-permute-done.21.refs_4_ = bf16[384,1024]{1,0:T(8,128)(2,1)S(1)} collective-permute-done((bf16[384,1024]{1,0:T(8,128)(2,1)S(1)}, bf16[384,1024]{1,0:T(8,128)(2,1)S(1)}, u32[]{:S(2)}, u32[]{:S(2)}) %collective-permute-start.21) | collective-permute-done | bytes 786464 | tf_op jit(solution)/shard_map/L_XM2a/ppermute | solution.py:286
  118.1 4.7 %collective-permute-start.19 = (bf16[384,1024]{1,0:T(8,128)(2,1)S(1)}, bf16[384,1024]{1,0:T(8,128)(2,1)S(1)}, u32[]{:S(2)}, u32[]{:S(2)}) collective-permute-start(bf16[384,1024]{1,0:T(8,128)(2,1)S(1)} %slice.11), channel_id=1, source_target_pairs={{0,8},{2,10},{4,12},{6,14},{8,0},{10,2},{12,4},{14,6},{16,24},{18,... | collective-permute-start | bytes 2359304 | tf_op jit(solution)/shard_map/L_E/ppermute | solution.py:286
  123.1 8.0 %shard_map.61 = bf16[2,192,512]{2,1,0:T(8,128)(2,1)S(1)} custom-call(s32[17]{0:T(128)S(1)} %get-tuple-element.63.blocks_ref, bf16[2,512,16384]{2,1,0:T(8,128)(2,1)} %s_ref.17, bf16[384,1024]{1,0:T(8,128)(2,1)S(1)} %shard_map.59.refs_0_, bf16[384,1024]{1,0:T(8,128)(2,1)S(1)} %collective-permute-done.24.refs_1_, ...), custom_call_target="tpu_custom_call" | custom-call | flops 1000 | bytes 1000 | tf_op jit(solution)/shard_map/pallas_call | solution.py:134
  131.1 1.6 %collective-permute-start.28 = (bf16[2,192,512]{2,1,0:T(8,128)(2,1)S(1)}, bf16[2,192,512]{2,1,0:T(8,128)(2,1)S(1)}, u32[]{:S(2)}, u32[]{:S(2)}) collective-permute-start(bf16[2,192,512]{2,1,0:T(8,128)(2,1)S(1)} %shard_map.61), channel_id=1, source_target_pairs={{0,1},{1,0},{2,3},{3,2},{4,5},{5,4},{6,7},{7,6},{8,9},{9,8},{10,11... | collective-permute-start | bytes 1179656 | tf_op jit(solution)/shard_map/L_partial/ppermute | solution.py:372
  132.7 6.2 %shard_map.60.refs_2_ = f32[384,1024]{1,0:T(8,128)S(1)} custom-call(s32[17]{0:T(128)S(1)} %get-tuple-element.63.blocks_ref, bf16[2,512,16384]{2,1,0:T(8,128)(2,1)} %s_ref.17, bf16[384,1024]{1,0:T(8,128)(2,1)S(1)} %collective-permute-done.20.refs_0_, bf16[384,1024]{1,0:T(8,128)(2,1)S(1)} %collective-permute-done.22.refs_1_, ...), custom_call_target="tpu_custom_call", output_to_operand_aliasing={{}: (6, {})} | custom-call | flops 1000 | bytes 1000 | tf_op jit(solution)/shard_map/pallas_call | solution.py:134
  138.9 1.7 %collective-permute-done.19.refs_1_ = bf16[384,1024]{1,0:T(8,128)(2,1)S(1)} collective-permute-done((bf16[384,1024]{1,0:T(8,128)(2,1)S(1)}, bf16[384,1024]{1,0:T(8,128)(2,1)S(1)}, u32[]{:S(2)}, u32[]{:S(2)}) %collective-permute-start.19) | collective-permute-done | bytes 786464 | tf_op jit(solution)/shard_map/L_E/ppermute | solution.py:286
  140.6 1.5 collective-permute-done.18.refs_0_
  142.6 1.9 %shard_map.62.refs_2_ = f32[384,1024]{1,0:T(8,128)S(1)} custom-call(bf16[4,2,512,1024]{3,2,1,0:T(8,128)(2,1)S(1)} %shard_map.57.tiles_ref, bf16[384,1024]{1,0:T(8,128)(2,1)S(1)} %collective-permute-done.18.refs_0_, bf16[384,1024]{1,0:T(8,128)(2,1)S(1)} %collective-permute-done.19.refs_1_, ...), custom_call_target="tpu_custom_call", output_to_operand_aliasing={{}: (3, {})} | custom-call | flops 1000 | bytes 1000 | tf_op jit(solution)/shard_map/pallas_call | solution.py:208
  144.5 1.0 collective-permute-done.30.refs_1_
  145.5 2.6 %shard_map.63 = bf16[2,192,512]{2,1,0:T(8,128)(2,1)} custom-call(bf16[4,2,512,1024]{3,2,1,0:T(8,128)(2,1)S(1)} %shard_map.57.tiles_ref, bf16[384,1024]{1,0:T(8,128)(2,1)S(1)} %collective-permute-done.29.refs_0_, bf16[384,1024]{1,0:T(8,128)(2,1)S(1)} %collective-permute-done.30.refs_1_, f32[384,1024]{1,0:T(8,128)S(1)} %shard_map.62.refs_2_, ...), custom_call_target="tpu_custom_call" | custom-call | flops 1000 | bytes 1000 | tf_op jit(solution)/shard_map/pallas_call | solution.py:208
  (37 shorter events, 3.5 us)
Async XLA Ops:
  3.7 27.0 %collective-permute-start.5 = (bf16[768,1024]{1,0:T(8,128)(2,1)}, bf16[768,1024]{1,0:T(8,128)(2,1)S(1)}, u32[]{:S(2)}, u32[]{:S(2)}) collective-permute-start(bf16[768,1024]{1,0:T(8,128)(2,1)} %get-tuple-element.45.refs_0_), channel_id=1, source_target_pairs={{0,2},{2,0},{4,6},{6,4},{8,10},{10,8},{12,14},{14,12},{16,18},{18,... | collective-permute-start | bytes 4718600 | tf_op jit(solution)/shard_map/L_CO/ppermute | solution.py:286
  4.1 9.2 %collective-permute-start.1 = (bf16[384,1024]{1,0:T(8,128)(2,1)}, bf16[384,1024]{1,0:T(8,128)(2,1)}, u32[]{:S(2)}, u32[]{:S(2)}) collective-permute-start(bf16[384,1024]{1,0:T(8,128)(2,1)} %get-tuple-element.42), channel_id=1, source_target_pairs={{8,16},{10,18},{12,20},{14,22},{16,8},{18,10},{20,12},{22,14},{9,1... | collective-permute-start | bytes 2359304 | tf_op jit(solution)/shard_map/L_Qa/ppermute | solution.py:286
  5.7 42.3 %collective-permute-start.4 = (bf16[768,1024]{1,0:T(8,128)(2,1)}, bf16[768,1024]{1,0:T(8,128)(2,1)S(1)}, u32[]{:S(2)}, u32[]{:S(2)}) collective-permute-start(bf16[768,1024]{1,0:T(8,128)(2,1)} %get-tuple-element.45.refs_0_), channel_id=1, source_target_pairs={{0,4},{2,6},{4,0},{6,2},{8,12},{10,14},{12,8},{14,10},{16,20},{18,... | collective-permute-start | bytes 4718600 | tf_op jit(solution)/shard_map/L_XO/ppermute | solution.py:286
  8.2 21.7 %collective-permute-start = (bf16[384,1024]{1,0:T(8,128)(2,1)}, bf16[384,1024]{1,0:T(8,128)(2,1)}, u32[]{:S(2)}, u32[]{:S(2)}) collective-permute-start(bf16[384,1024]{1,0:T(8,128)(2,1)} %get-tuple-element.42), channel_id=1, source_target_pairs={{0,8},{2,10},{4,12},{6,14},{8,0},{10,2},{12,4},{14,6},{16,24},{18,... | collective-permute-start | bytes 2359304 | tf_op jit(solution)/shard_map/L_Pa/ppermute | solution.py:286
  11.7 27.5 %collective-permute-start.3 = (bf16[384,1024]{1,0:T(8,128)(2,1)}, bf16[384,1024]{1,0:T(8,128)(2,1)}, u32[]{:S(2)}, u32[]{:S(2)}) collective-permute-start(bf16[384,1024]{1,0:T(8,128)(2,1)} %get-tuple-element.44), channel_id=1, source_target_pairs={{8,16},{10,18},{12,20},{14,22},{16,8},{18,10},{20,12},{22,14},{9,1... | collective-permute-start | bytes 2359304 | tf_op jit(solution)/shard_map/L_Qb/ppermute | solution.py:286
  13.3 34.7 %collective-permute-start.2 = (bf16[384,1024]{1,0:T(8,128)(2,1)}, bf16[384,1024]{1,0:T(8,128)(2,1)}, u32[]{:S(2)}, u32[]{:S(2)}) collective-permute-start(bf16[384,1024]{1,0:T(8,128)(2,1)} %get-tuple-element.44), channel_id=1, source_target_pairs={{0,8},{2,10},{4,12},{6,14},{8,0},{10,2},{12,4},{14,6},{16,24},{18,... | collective-permute-start | bytes 2359304 | tf_op jit(solution)/shard_map/L_Pb/ppermute | solution.py:286
  29.9 28.8 %collective-permute-start.7 = (bf16[384,1024]{1,0:T(8,128)(2,1)}, bf16[384,1024]{1,0:T(8,128)(2,1)S(1)}, u32[]{:S(2)}, u32[]{:S(2)}) collective-permute-start(bf16[384,1024]{1,0:T(8,128)(2,1)} %collective-permute-done.refs_0_), channel_id=1, source_target_pairs={{8,16},{10,18},{12,20},{14,22},{16,8},{18,10},{20,12},{22,14},{9,1... | collective-permute-start | bytes 2359304 | tf_op jit(solution)/shard_map/L_Ta/ppermute | solution.py:286
  30.7 34.1 %collective-permute-start.6 = (bf16[384,1024]{1,0:T(8,128)(2,1)}, bf16[384,1024]{1,0:T(8,128)(2,1)S(1)}, u32[]{:S(2)}, u32[]{:S(2)}) collective-permute-start(bf16[384,1024]{1,0:T(8,128)(2,1)} %collective-permute-done.1.first_ref), channel_id=1, source_target_pairs={{8,0},{10,2},{12,4},{14,6},{16,24},{18,26},{20,28},{22,30},{9,1},{... | collective-permute-start | bytes 2359304 | tf_op jit(solution)/shard_map/L_Sa/ppermute | solution.py:286
  32.0 1.4 copy-start
  48.0 17.0 %collective-permute-start.8 = (bf16[384,1024]{1,0:T(8,128)(2,1)}, bf16[384,1024]{1,0:T(8,128)(2,1)S(1)}, u32[]{:S(2)}, u32[]{:S(2)}) collective-permute-start(bf16[384,1024]{1,0:T(8,128)(2,1)} %collective-permute-done.refs_0_), channel_id=1, source_target_pairs={{0,4},{2,6},{4,0},{6,2},{8,12},{10,14},{12,8},{14,10},{16,20},{18,... | collective-permute-start | bytes 2359304 | tf_op jit(solution)/shard_map/L_XPa/ppermute | solution.py:286
  49.5 18.7 %collective-permute-start.14 = (bf16[768,1024]{1,0:T(8,128)(2,1)S(1)}, bf16[768,1024]{1,0:T(8,128)(2,1)S(1)}, u32[]{:S(2)}, u32[]{:S(2)}) collective-permute-start(bf16[768,1024]{1,0:T(8,128)(2,1)S(1)} %collective-permute-done.4.refs_1_), channel_id=1, source_target_pairs={{0,2},{2,0},{4,6},{6,4},{8,10},{10,8},{12,14},{14,12},{16,18},{18,... | collective-permute-start | bytes 4718600 | tf_op jit(solution)/shard_map/L_CXO/ppermute | solution.py:286
  50.1 30.5 %collective-permute-start.12 = (bf16[384,1024]{1,0:T(8,128)(2,1)}, bf16[384,1024]{1,0:T(8,128)(2,1)S(1)}, u32[]{:S(2)}, u32[]{:S(2)}) collective-permute-start(bf16[384,1024]{1,0:T(8,128)(2,1)} %collective-permute-done.3.first_ref), channel_id=1, source_target_pairs={{8,0},{10,2},{12,4},{14,6},{16,24},{18,26},{20,28},{22,30},{9,1},{... | collective-permute-start | bytes 2359304 | tf_op jit(solution)/shard_map/L_Sb/ppermute | solution.py:286
  65.6 16.6 %collective-permute-start.13 = (bf16[384,1024]{1,0:T(8,128)(2,1)S(1)}, bf16[384,1024]{1,0:T(8,128)(2,1)S(1)}, u32[]{:S(2)}, u32[]{:S(2)}) collective-permute-start(bf16[384,1024]{1,0:T(8,128)(2,1)S(1)} %shard_map.50.refs_1_), channel_id=1, source_target_pairs={{0,4},{2,6},{4,0},{6,2},{8,12},{10,14},{12,8},{14,10},{16,20},{18,... | collective-permute-start | bytes 2359304 | tf_op jit(solution)/shard_map/L_XM1a/ppermute | solution.py:286
  67.3 18.6 %collective-permute-start.16 = (bf16[768,1024]{1,0:T(8,128)(2,1)S(1)}, bf16[768,1024]{1,0:T(8,128)(2,1)S(1)}, u32[]{:S(2)}, u32[]{:S(2)}) collective-permute-start(bf16[768,1024]{1,0:T(8,128)(2,1)S(1)} %shard_map.54), channel_id=1, source_target_pairs={{0,2},{2,0},{4,6},{6,4},{8,10},{10,8},{12,14},{14,12},{16,18},{18,... | collective-permute-start | bytes 4718600 | tf_op jit(solution)/shard_map/L_CXPaM1a/ppermute | solution.py:286
  67.4 17.1 %collective-permute-start.9 = (bf16[384,1024]{1,0:T(8,128)(2,1)}, bf16[384,1024]{1,0:T(8,128)(2,1)S(1)}, u32[]{:S(2)}, u32[]{:S(2)}) collective-permute-start(bf16[384,1024]{1,0:T(8,128)(2,1)} %collective-permute-done.2.refs_1_), channel_id=1, source_target_pairs={{8,16},{10,18},{12,20},{14,22},{16,8},{18,10},{20,12},{22,14},{9,1... | collective-permute-start | bytes 2359304 | tf_op jit(solution)/shard_map/L_Tb/ppermute | solution.py:286
  72.1 25.4 %collective-permute-start.11 = (bf16[384,1024]{1,0:T(8,128)(2,1)S(1)}, bf16[384,1024]{1,0:T(8,128)(2,1)S(1)}, u32[]{:S(2)}, u32[]{:S(2)}) collective-permute-start(bf16[384,1024]{1,0:T(8,128)(2,1)S(1)} %collective-permute-done.7.first_ref), channel_id=1, source_target_pairs={{8,0},{10,2},{12,4},{14,6},{16,24},{18,26},{20,28},{22,30},{9,1},{... | collective-permute-start | bytes 2359304 | tf_op jit(solution)/shard_map/L_Ua/ppermute | solution.py:286
  82.9 16.2 %collective-permute-start.15 = (bf16[384,1024]{1,0:T(8,128)(2,1)S(1)}, bf16[384,1024]{1,0:T(8,128)(2,1)S(1)}, u32[]{:S(2)}, u32[]{:S(2)}) collective-permute-start(bf16[384,1024]{1,0:T(8,128)(2,1)S(1)} %shard_map.53.refs_0_), channel_id=1, source_target_pairs={{0,4},{2,6},{4,0},{6,2},{8,12},{10,14},{12,8},{14,10},{16,20},{18,... | collective-permute-start | bytes 2359304 | tf_op jit(solution)/shard_map/L_XM1b/ppermute | solution.py:286
  84.5 21.4 %collective-permute-start.17 = (bf16[384,1024]{1,0:T(8,128)(2,1)S(1)}, bf16[384,1024]{1,0:T(8,128)(2,1)S(1)}, u32[]{:S(2)}, u32[]{:S(2)}) collective-permute-start(bf16[384,1024]{1,0:T(8,128)(2,1)S(1)} %shard_map.53.refs_0_), channel_id=1, source_target_pairs={{0,2},{2,0},{4,6},{6,4},{8,10},{10,8},{12,14},{14,12},{16,18},{18,... | collective-permute-start | bytes 2359304 | tf_op jit(solution)/shard_map/L_CM1b/ppermute | solution.py:286
  84.5 29.4 %collective-permute-start.10 = (bf16[384,1024]{1,0:T(8,128)(2,1)S(1)}, bf16[384,1024]{1,0:T(8,128)(2,1)S(1)}, u32[]{:S(2)}, u32[]{:S(2)}) collective-permute-start(bf16[384,1024]{1,0:T(8,128)(2,1)S(1)} %collective-permute-done.9.first_ref), channel_id=1, source_target_pairs={{8,0},{10,2},{12,4},{14,6},{16,24},{18,26},{20,28},{22,30},{9,1},{... | collective-permute-start | bytes 2359304 | tf_op jit(solution)/shard_map/L_Ub/ppermute | solution.py:286
  99.8 17.2 %collective-permute-start.21 = (bf16[384,1024]{1,0:T(8,128)(2,1)S(1)}, bf16[384,1024]{1,0:T(8,128)(2,1)S(1)}, u32[]{:S(2)}, u32[]{:S(2)}) collective-permute-start(bf16[384,1024]{1,0:T(8,128)(2,1)S(1)} %shard_map.59.refs_0_), channel_id=1, source_target_pairs={{0,4},{2,6},{4,0},{6,2},{8,12},{10,14},{12,8},{14,10},{16,20},{18,... | collective-permute-start | bytes 2359304 | tf_op jit(solution)/shard_map/L_XM2a/ppermute | solution.py:286
  101.3 16.2 %collective-permute-start.24 = (bf16[384,1024]{1,0:T(8,128)(2,1)S(1)}, bf16[384,1024]{1,0:T(8,128)(2,1)S(1)}, u32[]{:S(2)}, u32[]{:S(2)}) collective-permute-start(bf16[384,1024]{1,0:T(8,128)(2,1)S(1)} %collective-permute-done.13.refs_2_), channel_id=1, source_target_pairs={{0,2},{2,0},{4,6},{6,4},{8,10},{10,8},{12,14},{14,12},{16,18},{18,... | collective-permute-start | bytes 2359304 | tf_op jit(solution)/shard_map/L_CXM1a/ppermute | solution.py:286
  101.3 16.8 %collective-permute-start.25 = (bf16[384,1024]{1,0:T(8,128)(2,1)S(1)}, bf16[384,1024]{1,0:T(8,128)(2,1)S(1)}, u32[]{:S(2)}, u32[]{:S(2)}) collective-permute-start(bf16[384,1024]{1,0:T(8,128)(2,1)S(1)} %shard_map.59.refs_0_), channel_id=1, source_target_pairs={{0,2},{2,0},{4,6},{6,4},{8,10},{10,8},{12,14},{14,12},{16,18},{18,... | collective-permute-start | bytes 2359304 | tf_op jit(solution)/shard_map/L_CM2a/ppermute | solution.py:286
  105.9 11.7 %collective-permute-start.26 = (bf16[384,1024]{1,0:T(8,128)(2,1)}, bf16[384,1024]{1,0:T(8,128)(2,1)S(1)}, u32[]{:S(2)}, u32[]{:S(2)}) collective-permute-start(bf16[384,1024]{1,0:T(8,128)(2,1)} %collective-permute-done.refs_0_), channel_id=1, source_target_pairs={{0,2},{2,0},{4,6},{6,4},{8,10},{10,8},{12,14},{14,12},{16,18},{18,... | collective-permute-start | bytes 2359304 | tf_op jit(solution)/shard_map/L_CPa/ppermute | solution.py:286
  117.0 5.8 %collective-permute-start.27 = (bf16[384,1024]{1,0:T(8,128)(2,1)S(1)}, bf16[384,1024]{1,0:T(8,128)(2,1)S(1)}, u32[]{:S(2)}, u32[]{:S(2)}) collective-permute-start(bf16[384,1024]{1,0:T(8,128)(2,1)S(1)} %collective-permute-done.21.refs_4_), channel_id=1, source_target_pairs={{0,2},{2,0},{4,6},{6,4},{8,10},{10,8},{12,14},{14,12},{16,18},{18,... | collective-permute-start | bytes 2359304 | tf_op jit(solution)/shard_map/L_CXM2a/ppermute | solution.py:286
  117.0 14.1 %collective-permute-start.20 = (bf16[384,1024]{1,0:T(8,128)(2,1)S(1)}, bf16[384,1024]{1,0:T(8,128)(2,1)S(1)}, u32[]{:S(2)}, u32[]{:S(2)}) collective-permute-start(bf16[384,1024]{1,0:T(8,128)(2,1)S(1)} %collective-permute-done.15.refs_2_), channel_id=1, source_target_pairs={{0,2},{2,0},{4,6},{6,4},{8,10},{10,8},{12,14},{14,12},{16,18},{18,... | collective-permute-start | bytes 2359304 | tf_op jit(solution)/shard_map/L_CXM1b/ppermute | solution.py:286
  117.5 15.1 %collective-permute-start.22 = (bf16[384,1024]{1,0:T(8,128)(2,1)}, bf16[384,1024]{1,0:T(8,128)(2,1)S(1)}, u32[]{:S(2)}, u32[]{:S(2)}) collective-permute-start(bf16[384,1024]{1,0:T(8,128)(2,1)} %collective-permute-done.2.refs_1_), channel_id=1, source_target_pairs={{0,2},{2,0},{4,6},{6,4},{8,10},{10,8},{12,14},{14,12},{16,18},{18,... | collective-permute-start | bytes 2359304 | tf_op jit(solution)/shard_map/L_CPb/ppermute | solution.py:286
  117.6 15.0 %collective-permute-start.23 = (bf16[384,1024]{1,0:T(8,128)(2,1)S(1)}, bf16[384,1024]{1,0:T(8,128)(2,1)S(1)}, u32[]{:S(2)}, u32[]{:S(2)}) collective-permute-start(bf16[384,1024]{1,0:T(8,128)(2,1)S(1)} %shard_map.58.refs_2_), channel_id=1, source_target_pairs={{0,2},{2,0},{4,6},{6,4},{8,10},{10,8},{12,14},{14,12},{16,18},{18,... | collective-permute-start | bytes 2359304 | tf_op jit(solution)/shard_map/L_CM2b/ppermute | solution.py:286
  118.1 22.5 %collective-permute-start.19 = (bf16[384,1024]{1,0:T(8,128)(2,1)S(1)}, bf16[384,1024]{1,0:T(8,128)(2,1)S(1)}, u32[]{:S(2)}, u32[]{:S(2)}) collective-permute-start(bf16[384,1024]{1,0:T(8,128)(2,1)S(1)} %slice.11), channel_id=1, source_target_pairs={{0,8},{2,10},{4,12},{6,14},{8,0},{10,2},{12,4},{14,6},{16,24},{18,... | collective-permute-start | bytes 2359304 | tf_op jit(solution)/shard_map/L_E/ppermute | solution.py:286
  122.8 19.3 %collective-permute-start.18 = (bf16[384,1024]{1,0:T(8,128)(2,1)S(1)}, bf16[384,1024]{1,0:T(8,128)(2,1)S(1)}, u32[]{:S(2)}, u32[]{:S(2)}) collective-permute-start(bf16[384,1024]{1,0:T(8,128)(2,1)S(1)} %shard_map.58.refs_2_), channel_id=1, source_target_pairs={{0,4},{2,6},{4,0},{6,2},{8,12},{10,14},{12,8},{14,10},{16,20},{18,... | collective-permute-start | bytes 2359304 | tf_op jit(solution)/shard_map/L_XM2b/ppermute | solution.py:286
  131.1 11.0 %collective-permute-start.28 = (bf16[2,192,512]{2,1,0:T(8,128)(2,1)S(1)}, bf16[2,192,512]{2,1,0:T(8,128)(2,1)S(1)}, u32[]{:S(2)}, u32[]{:S(2)}) collective-permute-start(bf16[2,192,512]{2,1,0:T(8,128)(2,1)S(1)} %shard_map.61), channel_id=1, source_target_pairs={{0,1},{1,0},{2,3},{3,2},{4,5},{5,4},{6,7},{7,6},{8,9},{9,8},{10,11... | collective-permute-start | bytes 1179656 | tf_op jit(solution)/shard_map/L_partial/ppermute | solution.py:372
  142.1 2.4 %collective-permute-start.29 = (bf16[384,1024]{1,0:T(8,128)(2,1)S(1)}, bf16[384,1024]{1,0:T(8,128)(2,1)S(1)}, u32[]{:S(2)}, u32[]{:S(2)}) collective-permute-start(bf16[384,1024]{1,0:T(8,128)(2,1)S(1)} %collective-permute-done.18.refs_0_), channel_id=1, source_target_pairs={{0,2},{2,0},{4,6},{6,4},{8,10},{10,8},{12,14},{14,12},{16,18},{18,... | collective-permute-start | bytes 2359304 | tf_op jit(solution)/shard_map/L_CXM2b/ppermute | solution.py:286
  142.1 3.4 %collective-permute-start.30 = (bf16[384,1024]{1,0:T(8,128)(2,1)S(1)}, bf16[384,1024]{1,0:T(8,128)(2,1)S(1)}, u32[]{:S(2)}, u32[]{:S(2)}) collective-permute-start(bf16[384,1024]{1,0:T(8,128)(2,1)S(1)} %collective-permute-done.19.refs_1_), channel_id=1, source_target_pairs={{0,2},{2,0},{4,6},{6,4},{8,10},{10,8},{12,14},{14,12},{16,18},{18,... | collective-permute-start | bytes 2359304 | tf_op jit(solution)/shard_map/L_CE/ppermute | solution.py:286
